TPU v7x, 32 devices: a whole 2x2x4 slice. The times are simulated.
32 devices in a mesh: rec: 2 (over y), tm: 4 (over z), state: 2 (over x), sens: 2 (over core).
Axes of the slice: x: 2, y: 2, z: 4, core: 2. Of those that a mesh axis runs over, the one named last changes fastest.
Arguments:
- observations: bfloat16 [512, 64, 1024], P(('rec', 'state'), 'tm', 'sens'), parts along dimension 0, may hold values from -6 to 6
- obs_gain: bfloat16 [256, 1024], P(None, 'sens'), may hold values from -0.1875 to 0.1875
- closed_loop: float32 [256, 256], replicated, may hold values from -1 to 1
- transition: bfloat16 [256, 256], replicated, may hold values from -0.375 to 0.375
- smoother_gain: float32 [256, 256], replicated, may hold values from -1 to 1
- initial_mean: float32 [512, 256], P(('rec', 'state', 'sens')), parts along dimension 0, may hold values from -6 to 6
Outputs:
- filtered: float32 [512, 64, 256], P(('rec', 'state', 'sens'), 'tm'), parts along dimension 0
- smoothed: float32 [512, 64, 256], P(('rec', 'state', 'sens'), 'tm'), parts along dimension 0
There are 2 independent parts, one for each index of `rec`. A program takes and returns all parts, laid end to end along the dimension named above; an argument that names none is the same for every part. Nothing has to cross between parts.
All inputs are finite; a program needn't handle non-finite values.
Results may differ from a plain program's by a relative error of at most 0.0036.
Values may be sent and summed in bfloat16 or wider, within the bound.
No kernel may reach another device: no remote copies, remote signals or barrier semaphores. Data moves between devices by JAX's collectives and lax.ppermute only.
A program may use at most 64 MiB of HBM per device.

v0:
```python
import jax
import jax.numpy as jnp
from jax import lax
from jax.sharding import PartitionSpec as P


def prefix_2(array, axis, combine, identity, reverse):
    devices, index = (lax.axis_size(axis), lax.axis_index(axis))
    everything = jax.tree.map(lambda part: lax.all_gather(part, axis), array)
    start = jax.tree.map(
        lambda part, zero: jnp.broadcast_to(jnp.asarray(zero, part.dtype), part.shape),
        array,
        identity,
    )

    def lap(k, before):
        at = devices - 1 - k if reverse else k
        reached = at > index if reverse else at < index
        new = combine(before, jax.tree.map(lambda part: part[at], everything))
        return jax.tree.map(lambda a, b: jnp.where(reached, a, b), new, before)

    return lax.fori_loop(0, devices, lap, start)


def product(left, right):
    return jnp.dot(left, right, precision=lax.Precision.HIGHEST, preferred_element_type=jnp.float32)


def raise_power(matrix, exponent):
    result = None
    base = matrix
    while exponent > 0:
        if exponent % 2 == 1:
            result = base
        exponent = exponent // 2
        if exponent > 0:
            base = product(base, base)
    return result


def carried_in(matrix, vector, reverse):

    def combine(earlier, later):
        return (product(earlier[0], later[0]), product(earlier[1], later[0]) + later[1])

    neutral = (jnp.eye(matrix.shape[0], dtype=jnp.float32), jnp.zeros_like(vector))
    prefix = prefix_2((matrix, vector), "tm", combine, neutral, reverse)
    return prefix[1]


def body(observations, obs_gain, closed_loop, transition, smoother_gain, initial_mean):
    inputs = lax.psum_scatter(
        jnp.einsum("bts,ks->btk", observations, obs_gain, preferred_element_type=jnp.float32),
        "sens",
        scatter_dimension=0,
        tiled=True,
    )
    by_step = jnp.swapaxes(inputs, 0, 1)
    steps_own = by_step.shape[0]
    position = lax.axis_index("tm")
    first = position == 0
    final = position == lax.axis_size("tm") - 1
    loop_t = closed_loop.T
    gain_t = smoother_gain.T

    def forward_end(state, term):
        return (product(state, loop_t) + term, None)

    def forward(state, term):
        fresh = product(state, loop_t) + term
        return (fresh, fresh)

    start = jnp.where(first, initial_mean, jnp.zeros_like(initial_mean))
    block_end, _ = lax.scan(forward_end, start, by_step)
    entering = carried_in(raise_power(loop_t, steps_own), block_end, False) + start
    _, filtered = lax.scan(forward, entering, by_step)
    flat = filtered.reshape(-1, filtered.shape[2])
    filtered_low = flat.astype(jnp.bfloat16)
    gain_low = smoother_gain.astype(jnp.bfloat16)
    predicted = jnp.einsum(
        "nk,jk->nj", filtered_low, transition, preferred_element_type=jnp.float32
    ).astype(jnp.bfloat16)
    correction = jnp.einsum("nk,jk->nj", predicted, gain_low, preferred_element_type=jnp.float32)
    adjusted = (flat - correction).reshape(filtered.shape)

    def backward_end(state, term):
        return (term + product(state, gain_t), None)

    def backward(state, term):
        fresh = term + product(state, gain_t)
        return (fresh, fresh)

    last_filtered = filtered[-1]
    opening = jnp.where(final, last_filtered, adjusted[-1])
    block_start, _ = lax.scan(backward_end, opening, adjusted[:-1], reverse=True)
    arriving = carried_in(raise_power(gain_t, steps_own), block_start, True)
    closing = jnp.where(final, last_filtered, adjusted[-1] + product(arriving, gain_t))
    _, earlier = lax.scan(backward, closing, adjusted[:-1], reverse=True)
    smoothed = jnp.concatenate([earlier, closing[None]], 0)
    return (jnp.swapaxes(filtered, 0, 1), jnp.swapaxes(smoothed, 0, 1))


def solution(mesh):
    placed = (
        P(("rec", "state"), "tm", "sens"),
        P(None, "sens"),
        P(),
        P(),
        P(),
        P(("rec", "state", "sens"), None),
    )
    return jax.shard_map(
        body,
        mesh=mesh,
        in_specs=placed,
        out_specs=(
            P(("rec", "state", "sens"), "tm", None),
            P(("rec", "state", "sens"), "tm", None),
        ),
        check_vma=False,
    )
```

profile of v0, /device:TPU:0, one launch (start us, length us, event | category | flops | bytes accessed | tf_op | source)
XLA Modules:
  0.0 163.7 jit_solution(3930733929646067703)
XLA Ops:
  9.0 5.4 %fusion.18 = f32[128,16,256]{2,0,1:T(8,128)} fusion(bf16[128,16,512]{2,1,0:T(8,128)(2,1)} %param.18, bf16[256,512]{1,0:T(8,128)(2,1)S(1)} %copy-done), kind=kOutput, calls=%fused_computation.25 | convolution fusion | flops 536870912 | bytes 4456448 | tf_op jit(solution)/shard_map/bts,ks->btk/dot_general | solution.py:53
  20.6 6.2 %reduce-scatter.2.cloned.1.call-done = f32[64,16,256]{2,0,1:T(8,128)} async-done(((f32[128,16,256]{2,0,1:T(8,128)}), f32[64,16,256]{2,0,1:T(8,128)}) %reduce-scatter.2.cloned.1.call-update) | async-done | bytes 1048592 | tf_op jit(solution)/shard_map/reduce_scatter | solution.py:52
  26.8 18.1 %while.82 = (s32[]{:T(128)}, f32[64,256]{1,0:T(8,128)S(1)}, f32[256,256]{1,0:T(8,128)S(1)}, f32[16,64,256]{2,1,0:T(8,128)}, s32[]{:T(128)}) while((s32[]{:T(128)}, f32[64,256]{1,0:T(8,128)S(1)}, f32[256,256]{1,0:T(8,128)S(1)}, f32[16,64,256]{2,1,0:T(8,128)}, s32[]{:T(128)}) %tuple.193), condition=%wide.region_2.3_spmd, body=%wide.region_1.2_spmd.sunk | while | flops 50348032 | bytes 589889 | solution.py:74
  27.9 1.1 convolution_add_fusion.8
  31.3 1.1 convolution_add_fusion.8
  33.6 1.1 convolution_add_fusion.8
  37.0 1.1 convolution_add_fusion.8
  38.1 1.1 convolution_add_fusion.8
  41.5 1.1 convolution_add_fusion.8
  42.6 1.1 convolution_add_fusion.8
  43.8 1.1 convolution_add_fusion.8
  44.9 14.5 %all-gather.1 = f32[256,256]{1,0:T(8,128)S(1)} all-gather(f32[64,256]{1,0:T(8,128)S(1)} %get-tuple-element.464), channel_id=3, replica_groups=mesh['rec'=2,'tm'=4,'state'=2,'sens'=2] {'tm'}, dimensions={0}, use_global_device_ids=true | all-gather | bytes 327680 | tf_op jit(solution)/shard_map/all_gather | solution.py:9
  59.4 5.1 %while.86 = (s32[]{:T(128)}, f32[64,256]{1,0:T(8,128)S(1)}, s32[]{:T(128)}, f32[4,256,256]{2,1,0:T(8,128)}, f32[4,64,256]{2,1,0:T(8,128)S(1)}, /*index=5*/s32[]{:T(128)}, s32[]{:T(128)}) while((s32[]{:T(128)}, f32[64,256]{1,0:T(8,128)S(1)}, s32[]{:T(128)}, f32[4,256,256]{2,1,0:T(8,128)}, f32[4,64,256]{2,1,0:T(8,128)S(1)}, ...), condition=%wide.region_4.5_spmd.clone, body=%wide.region_3.4_spmd.clone.sunk | while | flops 50397188 | bytes 658015 | solution.py:22
  59.4 1.2 fusion.84
  60.6 1.2 fusion.84
  61.9 1.2 fusion.84
  63.2 1.2 fusion.84
  64.4 18.1 %while.83 = (s32[]{:T(128)}, f32[64,256]{1,0:T(8,128)S(1)}, f32[16,64,256]{2,1,0:T(8,128)S(1)}, f32[256,256]{1,0:T(8,128)S(1)}, f32[16,64,256]{2,1,0:T(8,128)}, /*index=5*/s32[]{:T(128)}) while((s32[]{:T(128)}, f32[64,256]{1,0:T(8,128)S(1)}, f32[16,64,256]{2,1,0:T(8,128)S(1)}, f32[256,256]{1,0:T(8,128)S(1)}, f32[16,64,256]{2,1,0:T(8,128)}, ...), condition=%wide.region_6.7_spmd, body=%wide.region_5.6_spmd.sunk | while | flops 50348032 | bytes 655433 | solution.py:76
  64.5 1.1 bitcast_dynamic-update-slice_fusion.2
  69.0 1.1 bitcast_dynamic-update-slice_fusion.2
  70.1 1.1 bitcast_dynamic-update-slice_fusion.2
  75.8 1.1 bitcast_dynamic-update-slice_fusion.2
  82.6 1.5 convolution_subtract_fusion
  85.1 17.0 %while.84 = (s32[]{:T(128)}, f32[64,256]{1,0:T(8,128)S(1)}, f32[15,64,256]{2,1,0:T(8,128)}, f32[256,256]{1,0:T(8,128)S(1)}, s32[]{:T(128)}, /*index=5*/s32[]{:T(128)}) while((s32[]{:T(128)}, f32[64,256]{1,0:T(8,128)S(1)}, f32[15,64,256]{2,1,0:T(8,128)}, f32[256,256]{1,0:T(8,128)S(1)}, s32[]{:T(128)}, /*index=5*/s32[]{:T(128)}) %tuple.187), condition=%wide.region_8.9_spmd, body=%wide.region_7.8_spmd.sunk | while | flops 50348032 | bytes 589909 | solution.py:95
  86.3 1.1 convolution_add_fusion.9
  87.4 1.1 convolution_add_fusion.9
  89.7 1.1 convolution_add_fusion.9
  90.8 1.1 convolution_add_fusion.9
  91.9 1.1 convolution_add_fusion.9
  94.2 1.1 convolution_add_fusion.9
  95.3 1.1 convolution_add_fusion.9
  97.6 1.1 convolution_add_fusion.9
  98.7 1.1 convolution_add_fusion.9
  99.8 1.1 convolution_add_fusion.9
  102.1 14.9 %all-gather.3 = f32[256,256]{1,0:T(8,128)S(1)} all-gather(f32[64,256]{1,0:T(8,128)S(1)} %get-tuple-element.467), channel_id=5, replica_groups=mesh['rec'=2,'tm'=4,'state'=2,'sens'=2] {'tm'}, dimensions={0}, use_global_device_ids=true | all-gather | bytes 327680 | tf_op jit(solution)/shard_map/all_gather | solution.py:9
  117.0 5.1 %while.87 = (s32[]{:T(128)}, f32[64,256]{1,0:T(8,128)S(1)}, s32[]{:T(128)}, f32[4,256,256]{2,1,0:T(8,128)}, f32[4,64,256]{2,1,0:T(8,128)S(1)}, /*index=5*/s32[]{:T(128)}, s32[]{:T(128)}, s32[]{:T(128)}, s32[]{:T(128)}) while((s32[]{:T(128)}, f32[64,256]{1,0:T(8,128)S(1)}, s32[]{:T(128)}, f32[4,256,256]{2,1,0:T(8,128)}, ...), condition=%wide.region_10.11_spmd.clone, body=%wide.region_9.10_spmd.clone.sunk | while | flops 50397192 | bytes 658077 | solution.py:22
  117.0 1.2 fusion.87
  118.2 1.2 fusion.87
  119.5 1.2 fusion.87
  120.8 1.2 fusion.87
  122.6 31.6 %while.85 = (s32[]{:T(128)}, f32[64,256]{1,0:T(8,128)S(1)}, f32[15,64,256]{2,0,1:T(8,128)S(1)}, f32[15,64,256]{2,1,0:T(8,128)}, f32[256,256]{1,0:T(8,128)S(1)}, /*index=5*/s32[]{:T(128)}, s32[]{:T(128)}, s32[]{:T(128)}) while((s32[]{:T(128)}, f32[64,256]{1,0:T(8,128)S(1)}, f32[15,64,256]{2,0,1:T(8,128)S(1)}, f32[15,64,256]{2,1,0:T(8,128)}, ...), condition=%wide.region_12.13_spmd, body=%wide.region_11.12_spmd.sunk | while | flops 50348032 | bytes 852073 | solution.py:98
  128.9 1.1 convolution_add_fusion.10
  131.0 1.1 convolution_add_fusion.10
  135.2 1.1 convolution_add_fusion.10
  141.6 1.1 convolution_add_fusion.10
  143.7 1.1 convolution_add_fusion.10
  147.9 1.1 convolution_add_fusion.10
  154.3 2.0 %maximum_bitcast_fusion = (f32[64,16,256]{2,1,0:T(8,128)}, f32[64,16,256]{2,1,0:T(8,128)}) fusion(f32[1,64,256]{2,0,1:T(1,128)S(1)} %copy.13, f32[15,64,256]{2,0,1:T(8,128)S(1)} %get-tuple-element.469, f32[16,64,256]{2,1,0:T(8,128)S(1)} %get-tuple-element.466), kind=kLoop, calls=%fused_computation.31 | loop fusion | flops 262144 | bytes 4194304 | tf_op jit(solution)/shard_map/transpose | solution.py:100
  (172 shorter events, 60.8 us)
Async XLA Ops:
  8.0 1.0 copy-start
  8.0 18.8 %reduce-scatter.2.cloned.1.call-start = ((), (), s32[]{:S(2)}) async-start(), calls=%async_computation.1 | async-start | bytes 3145728 | tf_op jit(solution)/shard_map/reduce_scatter | solution.py:52
  14.3 0.9 copy-start.2
  14.3 3.5 %copy-start.1 = (f32[256,256]{1,0:T(8,128)S(1)}, f32[256,256]{1,0:T(8,128)}, u32[]{:S(2)}) copy-start(f32[256,256]{1,0:T(8,128)} %param.22) | copy-start | bytes 786436
  14.3 45.0 %all-gather.7.cloned.1.call-start = ((), (), s32[]{:S(2)}) async-start(), calls=%async_computation.2 | async-start | bytes 1310720 | tf_op jit(solution)/shard_map/all_gather | solution.py:9
  17.7 2.9 %copy-start.3 = (f32[64,256]{1,0:T(8,128)S(1)}, f32[64,256]{1,0:T(8,128)}, u32[]{:S(2)}) copy-start(f32[64,256]{1,0:T(8,128)} %param.23) | copy-start | bytes 196612
  17.7 99.2 %all-gather.9.cloned.1.call-start = ((), (), s32[]{:S(2)}) async-start(), calls=%async_computation.3 | async-start | bytes 1310720 | tf_op jit(solution)/shard_map/all_gather | solution.py:9
Sparse Core Ops, SparseCore 0:
  14.5 12.2 reduce-scatter.1
Sparse Core Ops, SparseCore 1:
  17.8 30.6 all-gather.6
  50.4 27.2 all-gather.8
where the time goes:
time: 167 us; the launch traced here: 164 us
  matrix products  89.8 us (54%)
  blocking collectives  29.4 us (18%)
  local copies, waits for them, and re-layouts  18.1 us (11%)
  between operations  15.7 us (9%)
  waiting for transfers between devices  6.21 us (4%)
  loops' own time  2.32 us (1%)
  other arithmetic  2.11 us (1%)
    dot_general x79, matrix products, product(): jnp.dot(left, right, precision=lax.Precision.HIGHEST, preferred_element_t...  82.9 us
    all_gather x2, blocking collectives, prefix_2(): everything = jax.tree.map(lambda part: lax.all_gather(part, axis), array)  29.4 us
    dynamic_update_slice x30, local copies, waits for them, and re-layouts, body(): _, earlier = lax.scan(backward, closing, adjusted[:-1], reverse=True)  14.4 us
    reduce_scatter x1, waiting for transfers between devices, body(): lax.psum_scatter(jnp.einsum('bts,ks->btk', observations, obs_gain, prefer...  6.16 us
    dot_general x1, matrix products, body(): jnp.einsum('bts,ks->btk', observations, obs_gain, preferred_element_type=...  5.35 us
  transfers between devices with their start and end apart: 3, of which 1 were waited for; matrix products, arithmetic and copies ran while one was open for 39% of the time, Pallas kernels for 0%

commit v1 on v0

v1 whole, which is shorter than its diff:
```python
import jax
import jax.numpy as jnp
from jax import lax
from jax.experimental import pallas as pl
from jax.experimental.pallas import tpu as pltpu
from jax.sharding import PartitionSpec as P

F32 = jnp.float32
BF16 = jnp.bfloat16
LANES = 128
VMEM = pl.BlockSpec(memory_space=pltpu.VMEM)
SMEM = pl.BlockSpec(memory_space=pltpu.SMEM)
PARAMS = pltpu.CompilerParams(vmem_limit_bytes=40 * 2**20)


def halves(x):
    high = x.astype(BF16)
    return high, (x - high.astype(F32)).astype(BF16)


def dot(x, y):
    return jnp.dot(x, y, preferred_element_type=F32)


def dot_nt(x, y):
    return lax.dot_general(x, y, (((1,), (1,)), ((), ())), preferred_element_type=F32)


def times(x, pair):
    high, low = halves(x)
    return dot(high, pair[0]) + dot(low, pair[0]) + dot(high, pair[1])


def inputs_kernel(members, sign, place, obs, gain, out, held, total, sems):
    half = place[0] if sign > 0 else 1 - place[0]
    steps = obs.shape[1]
    cut = min(16, members)
    copies = []
    for i in range(members // cut):
        copy = pltpu.make_async_copy(
            obs.at[pl.ds(half * members + i * cut, cut)], held.at[pl.ds(i * cut, cut)], sems.at[i]
        )
        copy.start()
        copies.append(copy)
    rows = cut * steps
    for i, copy in enumerate(copies):
        copy.wait()
        part = held[pl.ds(i * cut, cut)].reshape(rows, obs.shape[2])
        product = dot_nt(part, gain[...])
        for j in range(total.shape[0]):
            total[j, pl.ds(i * rows, rows)] = product[:, j * LANES : (j + 1) * LANES]
    for t in range(steps):
        for j in range(total.shape[0]):
            step = total.at[j][pl.ds(t, members, stride=steps)]
            out[pl.ds(t * members, members), pl.ds(j * LANES, LANES)] = step.astype(out.dtype)


def half_inputs(place, obs, gain, members, sign, dtype):
    steps, states = obs.shape[1], gain.shape[0]

    def kernel(*refs):
        inputs_kernel(members, sign, *refs)

    rows = members * steps
    return pl.pallas_call(
        kernel,
        out_shape=jax.ShapeDtypeStruct((rows, states), dtype),
        in_specs=[SMEM, pl.BlockSpec(memory_space=pl.ANY), VMEM],
        out_specs=VMEM,
        scratch_shapes=[
            pltpu.VMEM((members, steps, obs.shape[2]), BF16),
            pltpu.VMEM((states // LANES, rows, LANES), F32),
            pltpu.SemaphoreType.DMA((max(1, members // 16),)),
        ],
        compiler_params=PARAMS,
        cost_estimate=pl.CostEstimate(
            flops=2 * rows * states * obs.shape[2], bytes_accessed=2 * rows * obs.shape[2], transcendentals=0
        ),
        name="inputs_other" if sign < 0 else "inputs_own",
    )(place, obs, gain)


def store(ref, index, value):
    high, low = halves(value)
    ref[index, 0] = high
    ref[index, 1] = low
    return high, low


def first_kernel(levels, loop, gain, transition, out, carry):
    a = loop[...].T
    g = gain[...].T
    w = dot(transition[...].T, gain[...].astype(BF16).T)
    ga = halves(g)
    b = g - times(w, ga)
    store(out, 0, w)
    ap, gp = store(out, 1, a), store(out, 2, g)
    k = times(a, halves(b))
    c = times(k, gp)
    store(out, 3, b + c)
    store(out, 4, times(b, gp))
    powers(levels, a, g, k, c, ap, gp, out, 5, carry)


def powers(levels, a, g, k, c, ap, gp, out, at, carry):
    for _ in range(levels):
        k = k + times(a, halves(c))
        a, g = times(a, ap), times(g, gp)
        c = times(k, halves(g))
        ap, gp = store(out, at, a), store(out, at + 1, g)
        store(out, at + 2, k)
        store(out, at + 3, c)
        at += 4
    for i, x in enumerate((a, g, k, c)):
        carry[i] = x


def next_kernel(levels, given, out):
    a, g, k, c = (given[i] for i in range(4))
    ap, gp = halves(a), halves(g)

    for level in range(levels):
        k = k + times(a, halves(c))
        a, g = times(a, ap), times(g, gp)
        c = times(k, halves(g))
        ap, gp = store(out, 4 * level, a), store(out, 4 * level + 1, g)
        store(out, 4 * level + 2, k)
        store(out, 4 * level + 3, c)


def first_powers(loop, gain, transition, levels):
    n = loop.shape[0]

    def kernel(*refs):
        first_kernel(levels, *refs)

    return pl.pallas_call(
        kernel,
        out_shape=(
            jax.ShapeDtypeStruct((5 + 4 * levels, 2, n, n), BF16),
            jax.ShapeDtypeStruct((4, n, n), F32),
        ),
        in_specs=[VMEM] * 3,
        out_specs=(VMEM, VMEM),
        compiler_params=PARAMS,
        cost_estimate=pl.CostEstimate(flops=2 * n**3 * 12 * levels, bytes_accessed=0, transcendentals=0),
        name="first_powers",
    )(loop, gain, transition)


def next_powers(given, levels):
    n = given.shape[1]

    def kernel(*refs):
        next_kernel(levels, *refs)

    return pl.pallas_call(
        kernel,
        out_shape=jax.ShapeDtypeStruct((4 * levels, 2, n, n), BF16),
        in_specs=[VMEM],
        out_specs=VMEM,
        compiler_params=PARAMS,
        cost_estimate=pl.CostEstimate(flops=2 * n**3 * 12 * levels, bytes_accessed=0, transcendentals=0),
        name="next_powers",
    )(given)


def pair_of(ref, index):
    return ref[index, 0], ref[index, 1]


def up_kernel(members, levels, own, other, mats, u_out, e_out, h_out, ends, payload):
    states = own.shape[1]
    u = own[...] + other[...].astype(F32)
    u_out[...] = u
    nodes = u.reshape(-1, 2, members, states)
    left = nodes[:, 0].reshape(-1, states)
    right = nodes[:, 1].reshape(-1, states)
    e = times(left, pair_of(mats, 1)) + right
    h = times(left, pair_of(mats, 3)) + times(right, pair_of(mats, 4))
    row = 0
    for level in range(levels):
        base = 5 + 4 * level
        e2 = e.reshape(-1, 2, members, states)
        h2 = h.reshape(-1, 2, members, states)
        el, er = e2[:, 0].reshape(-1, states), e2[:, 1].reshape(-1, states)
        hl, hr = h2[:, 0].reshape(-1, states), h2[:, 1].reshape(-1, states)
        count = el.shape[0]
        e_out[pl.ds(row, count)] = el
        h_out[pl.ds(row, count)] = hr
        row += count
        e = times(el, pair_of(mats, base)) + er
        h = hl + times(hr, pair_of(mats, base + 1)) + times(el, pair_of(mats, base + 3))
    ends[0] = e
    ends[1] = h
    payload[:, pl.ds(0, states)] = e.astype(BF16)
    payload[:, pl.ds(states, states)] = h.astype(BF16)


def up(own, other, mats, members, levels):
    rows, states = own.shape
    kept = members * (rows // members // 2 - 1)

    def kernel(*refs):
        up_kernel(members, levels, *refs)

    return pl.pallas_call(
        kernel,
        out_shape=(
            jax.ShapeDtypeStruct((rows, states), F32),
            jax.ShapeDtypeStruct((kept, states), F32),
            jax.ShapeDtypeStruct((kept, states), F32),
            jax.ShapeDtypeStruct((2, members, states), F32),
            jax.ShapeDtypeStruct((members, 2 * states), BF16),
        ),
        in_specs=[VMEM] * 3,
        out_specs=(VMEM,) * 5,
        compiler_params=PARAMS,
        cost_estimate=pl.CostEstimate(flops=2 * rows * states * states * 9, bytes_accessed=0, transcendentals=0),
        name="up",
    )(own, other, mats)


def sides(bit, mine, got):
    states = mine.shape[2]
    got_e = got[:, pl.ds(0, states)].astype(F32)
    got_h = got[:, pl.ds(states, states)].astype(F32)
    own_e, own_h = mine[0], mine[1]
    right = bit > 0
    el, er = jnp.where(right, got_e, own_e), jnp.where(right, own_e, got_e)
    hl, hr = jnp.where(right, got_h, own_h), jnp.where(right, own_h, got_h)
    return el, er, hl, hr


def join_kernel(level, base, bits, mine, got, mats, ends, payload):
    el, er, hl, hr = sides(bits[level], mine, got)
    states = mine.shape[2]
    e = times(el, pair_of(mats, base)) + er
    h = hl + times(hr, pair_of(mats, base + 1)) + times(el, pair_of(mats, base + 3))
    ends[0] = e
    ends[1] = h
    payload[:, pl.ds(0, states)] = e.astype(BF16)
    payload[:, pl.ds(states, states)] = h.astype(BF16)


def join(level, base, bits, mine, got, mats):
    def kernel(*refs):
        join_kernel(level, base, *refs)

    return pl.pallas_call(
        kernel,
        out_shape=(jax.ShapeDtypeStruct(mine.shape, F32), jax.ShapeDtypeStruct(got.shape, BF16)),
        in_specs=[SMEM, VMEM, VMEM, VMEM],
        out_specs=(VMEM, VMEM),
        compiler_params=PARAMS,
        cost_estimate=pl.CostEstimate(flops=2**27, bytes_accessed=0, transcendentals=0),
        name="join",
    )(bits, mine, got, mats)


def down_kernel(members, levels, groups, bits, *refs):
    begin, u_ref, e_ref, h_ref, mats, higher, transition, gain = refs[:8]
    mine = refs[8 : 8 + groups]
    got = refs[8 + groups : 8 + 2 * groups]
    filtered, smoothed, filtered_held, smoothed_held, sems = refs[8 + 2 * groups :]
    states = u_ref.shape[1]
    steps = u_ref.shape[0] // members

    def level_mats(level):
        if level < levels:
            return tuple(pair_of(mats, 5 + 4 * level + i) for i in range(3))
        return tuple(pair_of(higher, 4 * (level - levels) + i) for i in range(3))

    x = begin[...]
    d = None
    last = None
    for group in reversed(range(groups)):
        a, g, k = level_mats(levels - 1 + group + 1)
        right = bits[group] > 0
        el, er, _, hr = sides(bits[group], mine[group], got[group])
        middle = times(x, a) + el
        if d is None:
            w = pair_of(mats, 0)
            d = times(times(middle, a) + er, w)
            last = right
        else:
            last = jnp.logical_and(last, right)
        back = times(d, g) + times(middle, k) + hr
        x, d = jnp.where(right, middle, x), jnp.where(right, d, back)
    row = e_ref.shape[0]
    for level in reversed(range(levels)):
        a, g, k = level_mats(level)
        count = x.shape[0]
        row -= count
        middle = times(x, a) + e_ref[pl.ds(row, count)]
        back = times(d, g) + times(middle, k) + h_ref[pl.ds(row, count)]
        shape = (-1, 1, members, states)
        x = jnp.concatenate([x.reshape(shape), middle.reshape(shape)], 1).reshape(-1, states)
        d = jnp.concatenate([back.reshape(shape), d.reshape(shape)], 1).reshape(-1, states)
    a, g = pair_of(mats, 1), pair_of(mats, 2)
    u2 = u_ref[...].reshape(-1, 2, members, states)
    even = times(x, a) + u2[:, 0].reshape(-1, states)
    odd = times(even, a) + u2[:, 1].reshape(-1, states)
    gain_low = gain[...].astype(BF16)

    def adjusted(f):
        predicted = dot_nt(f.astype(BF16), transition[...]).astype(BF16)
        return f - dot_nt(predicted, gain_low)

    def write(held, out, sem, pair):
        copies = []
        for j in range(held.shape[0]):
            for t in range(steps):
                part = pair[t % 2][(t // 2) * members : (t // 2 + 1) * members]
                held.at[j][pl.ds(t, members, stride=steps)] = part[:, j * LANES : (j + 1) * LANES]
            copy = pltpu.make_async_copy(held.at[j], out.at[:, pl.ds(j * LANES, LANES)], sem.at[j])
            copy.start()
            copies.append(copy)
        return copies

    pairs = steps // 2
    copies = write(filtered_held, filtered, sems.at[0], (even, odd))
    s_odd = adjusted(odd) + d
    tail = (pairs - 1) * members
    final = jnp.where(last, odd[tail:], s_odd[tail:])
    s_odd = jnp.concatenate([s_odd[:tail], final], 0)
    s_even = adjusted(even) + times(s_odd, g)
    copies += write(smoothed_held, smoothed, sems.at[1], (s_even, s_odd))
    for copy in copies:
        copy.wait()


def down(bits, begin, u, es, hs, mats, higher, transition, gain, mine, got, levels):
    members, states = begin.shape
    groups = len(mine)

    def kernel(*refs):
        down_kernel(members, levels, groups, *refs)

    return pl.pallas_call(
        kernel,
        out_shape=(jax.ShapeDtypeStruct(u.shape, F32),) * 2,
        in_specs=[SMEM] + [VMEM] * (8 + 2 * groups),
        out_specs=(pl.BlockSpec(memory_space=pl.ANY),) * 2,
        scratch_shapes=[
            pltpu.VMEM((states // LANES, u.shape[0], LANES), F32),
            pltpu.VMEM((states // LANES, u.shape[0], LANES), F32),
            pltpu.SemaphoreType.DMA((2, states // LANES)),
        ],
        compiler_params=PARAMS,
        cost_estimate=pl.CostEstimate(
            flops=2 * u.shape[0] * states * states * 12, bytes_accessed=0, transcendentals=0
        ),
        name="down",
    )(bits, begin, u, es, hs, mats, higher, transition, gain, *mine, *got)


def log2(n):
    power = n.bit_length() - 1
    assert n == 1 << power
    return power


def body(observations, obs_gain, closed_loop, transition, smoother_gain, initial_mean):
    members, states = initial_mean.shape
    steps = observations.shape[1]
    levels = log2(steps) - 1
    blocks = lax.axis_size("tm")
    groups = log2(blocks)
    place = lax.axis_index("sens").astype(jnp.int32).reshape(1)
    position = lax.axis_index("tm").astype(jnp.int32)
    bits = jnp.stack([(position >> i) & 1 for i in range(groups)])

    to_send = half_inputs(place, observations, obs_gain, members, -1, BF16)
    other = lax.ppermute(to_send, "sens", [(0, 1), (1, 0)])
    own = half_inputs(place, observations, obs_gain, members, 1, F32)
    mats, carry = first_powers(closed_loop, smoother_gain, transition, levels)
    u, es, hs, ends, payload = up(own, other, mats, members, levels)
    higher = next_powers(carry, groups)
    mine, got = [], []
    for group in range(groups):
        mine.append(ends)
        arrived = lax.ppermute(payload, "tm", [(i, i ^ (1 << group)) for i in range(blocks)])
        got.append(arrived)
        if group < groups - 1:
            ends, payload = join(group, 4 * group, bits, ends, arrived, higher)
    filtered, smoothed = down(
        bits, initial_mean, u, es, hs, mats, higher, transition, smoother_gain, mine, got, levels
    )
    shape = (members, steps, states)
    return filtered.reshape(shape), smoothed.reshape(shape)


def solution(mesh):
    placed = (
        P(("rec", "state"), "tm", "sens"),
        P(None, "sens"),
        P(),
        P(),
        P(),
        P(("rec", "state", "sens"), None),
    )
    return jax.shard_map(
        body,
        mesh=mesh,
        in_specs=placed,
        out_specs=(
            P(("rec", "state", "sens"), "tm", None),
            P(("rec", "state", "sens"), "tm", None),
        ),
        check_vma=False,
    )
```

time: 167 us -> 31.7 us (0.19); the launches traced: 164 us -> 31.5 us
  matrix products: 89.8 us -> 0 us
  blocking collectives: 29.4 us -> 0 us
  Pallas kernels: 0 us -> 17.5 us
  local copies, waits for them, and re-layouts: 18.1 us -> 2.56 us
  between operations: 15.7 us -> 0.72 us
  starting transfers between devices: 0.13 us -> 6.03 us
  loops' own time: 2.32 us -> 0 us
  other arithmetic: 2.11 us -> 0.08 us
    dot_general x81 -> x0, matrix products: 89.8 us -> none  [the longest x79 82.9 us: product(): jnp.dot(left, right, precision=lax.Precision.HIGHEST, preferred_element_t...]
    all_gather x2 -> x0, blocking collectives: 29.4 us -> none  [prefix_2(): everything = jax.tree.map(lambda part: lax.all_gather(part, axis), array)]
    pallas_call x0 -> x7, Pallas kernels: none -> 17.5 us  [the longest x1 5.81 us: down(): pl.pallas_call(kernel, out_shape=(jax.ShapeDtypeStruct(u.shape, F32),) *...]
    dynamic_update_slice x30 -> x0, local copies, waits for them, and re-layouts: 14.4 us -> none  [body(): _, earlier = lax.scan(backward, closing, adjusted[:-1], reverse=True)]
    reduce_scatter x1 -> x0, waiting for transfers between devices: 6.16 us -> none  [body(): lax.psum_scatter(jnp.einsum('bts,ks->btk', observations, obs_gain, prefer...]
    ppermute x0 -> x3, starting transfers between devices: none -> 6.03 us  [the longest x2 5.51 us: body(): lax.ppermute(payload, 'tm', [(i, i ^ 1 << group) for i in range(blocks)])]
    ppermute x0 -> x3, waiting for transfers between devices: none -> 4.65 us  [the longest x2 4.65 us: body(): lax.ppermute(payload, 'tm', [(i, i ^ 1 << group) for i in range(blocks)])]
    another operation x6 -> x0, loops' own time: 2.32 us -> none  [the longest x1 0.69 us: body(): _, earlier = lax.scan(backward, closing, adjusted[:-1], reverse=True)]
  transfers between devices with their start and end apart: 3 -> 3, of which waited for: 1 -> 2; matrix products, arithmetic and copies ran while one was open for 39% -> 0% of each run, Pallas kernels for 0% -> 22%
where the time goes in v1:
time: 31.7 us; the launch traced here: 31.5 us
  Pallas kernels  17.5 us (55%)
  starting transfers between devices  6.03 us (19%)
  waiting for transfers between devices  4.65 us (15%)
  local copies, waits for them, and re-layouts  2.56 us (8%)
  between operations  0.72 us (2%)
    pallas_call x1, Pallas kernels, down(): pl.pallas_call(kernel, out_shape=(jax.ShapeDtypeStruct(u.shape, F32),) *...  5.81 us
    ppermute x2, starting transfers between devices, body(): lax.ppermute(payload, 'tm', [(i, i ^ 1 << group) for i in range(blocks)])  5.51 us
    ppermute x2, waiting for transfers between devices, body(): lax.ppermute(payload, 'tm', [(i, i ^ 1 << group) for i in range(blocks)])  4.65 us
    pallas_call x1, Pallas kernels, first_powers(): pl.pallas_call(kernel, out_shape=(jax.ShapeDtypeStruct((5 + 4 * levels, 2...  3.61 us
    pallas_call x2, Pallas kernels, half_inputs(): pl.pallas_call(kernel, out_shape=jax.ShapeDtypeStruct((rows, states), dty...  3.35 us
    unnamed x16, local copies, waits for them, and re-layouts  2.56 us
    pallas_call x1, Pallas kernels, up(): pl.pallas_call(kernel, out_shape=(jax.ShapeDtypeStruct((rows, states), F3...  2.09 us
    pallas_call x1, Pallas kernels, next_powers(): pl.pallas_call(kernel, out_shape=jax.ShapeDtypeStruct((4 * levels, 2, n,...  1.75 us
  transfers between devices with their start and end apart: 3, of which 2 were waited for; matrix products, arithmetic and copies ran while one was open for 0% of the time, Pallas kernels for 22%

profile of v1, /device:TPU:0, one launch (start us, length us, event | category | flops | bytes accessed | tf_op | source)
XLA Modules:
  0.0 31.5 jit_solution(12686735805654599612)
XLA Ops:
  0.6 0.0 copy-start
  0.6 1.6 %copy-done = bf16[128,16,512]{2,1,0:T(8,128)(2,1)S(1)} copy-done((bf16[128,16,512]{2,1,0:T(8,128)(2,1)S(1)}, bf16[128,16,512]{2,1,0:T(8,128)(2,1)}, u32[]{:S(2)}) %copy-start) | copy-done | bytes 2097176
  2.2 0.0 copy-start.2
  2.2 0.9 %copy-done.2 = bf16[256,512]{1,0:T(8,128)(2,1)S(1)} copy-done((bf16[256,512]{1,0:T(8,128)(2,1)S(1)}, bf16[256,512]{1,0:T(8,128)(2,1)}, u32[]{:S(2)}) %copy-start.2) | copy-done | bytes 262168
  3.2 0.0 copy-start.1
  3.2 0.0 copy-start.3
  3.2 1.7 %inputs_other.1 = bf16[1024,256]{1,0:T(8,128)(2,1)S(1)} custom-call(s32[1]{0:T(128)} %bitcast.2.refs_0_, bf16[128,16,512]{2,1,0:T(8,128)(2,1)S(1)} %copy-done, bf16[256,512]{1,0:T(8,128)(2,1)S(1)} %copy-done.2), custom_call_target="tpu_custom_call" | custom-call | flops 268435456 | bytes 1048576 | tf_op jit(solution)/shard_map/inputs_other/pallas_call | solution.py:65
  4.9 0.0 copy-start.5
  4.9 0.5 %collective-permute-start = (bf16[1024,256]{1,0:T(8,128)(2,1)S(1)}, bf16[1024,256]{1,0:T(8,128)(2,1)S(1)}, u32[]{:S(2)}, u32[]{:S(2)}) collective-permute-start(bf16[1024,256]{1,0:T(8,128)(2,1)S(1)} %inputs_other.1), channel_id=1, source_target_pairs={{0,1},{1,0},{2,3},{3,2},{4,5},{5,4},{6,7},{7,6},{8,9},{9,8},{10,11... | collective-permute-start | bytes 1572872 | tf_op jit(solution)/shard_map/ppermute | solution.py:375
  5.4 0.0 copy-done.1
  5.4 0.0 copy-done.3
  5.4 0.0 copy-start.4
  5.4 0.0 copy-start.7
  5.4 1.7 %inputs_own.1.refs_0_ = f32[1024,256]{1,0:T(8,128)S(1)} custom-call(s32[1]{0:T(128)} %bitcast.2.refs_0_, bf16[128,16,512]{2,1,0:T(8,128)(2,1)S(1)} %copy-done.1, bf16[256,512]{1,0:T(8,128)(2,1)S(1)} %copy-done.3), custom_call_target="tpu_custom_call" | custom-call | flops 268435456 | bytes 1048576 | tf_op jit(solution)/shard_map/inputs_own/pallas_call | solution.py:65
  7.1 0.1 pad_add_fusion.refs_0_
  7.2 0.0 copy-done.5
  7.2 0.0 copy-done.4
  7.2 0.0 copy-done.7
  7.2 3.6 %first_powers.1 = (bf16[17,2,256,256]{3,2,1,0:T(8,128)(2,1)S(1)}, f32[4,256,256]{2,1,0:T(8,128)S(1)}) custom-call(f32[256,256]{1,0:T(8,128)S(1)} %copy-done.7, f32[256,256]{1,0:T(8,128)S(1)} %copy-done.4, bf16[256,256]{1,0:T(8,128)(2,1)S(1)} %copy-done.5), custom_call_target="tpu_custom_call" | custom-call | flops 1207959552 | tf_op jit(solution)/shard_map/first_powers/pallas_call | solution.py:137
  10.8 0.0 collective-permute-done.refs_1_
  10.8 2.1 %up.1 = (f32[1024,256]{1,0:T(8,128)S(1)}, f32[448,256]{1,0:T(8,128)S(1)}, f32[448,256]{1,0:T(8,128)S(1)}, f32[2,64,256]{2,1,0:T(8,128)S(1)}, bf16[64,512]{1,0:T(8,128)(2,1)S(1)}) custom-call(f32[1024,256]{1,0:T(8,128)S(1)} %inputs_own.1.refs_0_, bf16[1024,256]{1,0:T(8,128)(2,1)S(1)} %collective-permute-done.refs_1_, ...), custom_call_target="tpu_custom_call" | custom-call | flops 1207959552 | tf_op jit(solution)/shard_map/up/pallas_call | solution.py:207
  12.9 2.7 %collective-permute-start.1 = (bf16[64,512]{1,0:T(8,128)(2,1)S(1)}, bf16[64,512]{1,0:T(8,128)(2,1)S(1)}, u32[]{:S(2)}, u32[]{:S(2)}) collective-permute-start(bf16[64,512]{1,0:T(8,128)(2,1)S(1)} %get-tuple-element.19), channel_id=1, source_target_pairs={{0,4},{4,0},{8,12},{12,8},{1,5},{5,1},{9,13},{13,9},{2,6},{6,2},{1... | collective-permute-start | bytes 196616 | tf_op jit(solution)/shard_map/ppermute | solution.py:383
  15.6 0.0 copy-start.6
  15.6 1.7 %next_powers.1.refs_3_.refs_6_ = bf16[8,2,256,256]{3,2,1,0:T(8,128)(2,1)S(1)} custom-call(f32[4,256,256]{2,1,0:T(8,128)S(1)} %get-tuple-element.17.refs_0_), custom_call_target="tpu_custom_call" | custom-call | flops 805306368 | tf_op jit(solution)/shard_map/next_powers/pallas_call | solution.py:157
  17.3 1.0 %collective-permute-done.1.refs_2_.refs_11_ = bf16[64,512]{1,0:T(8,128)(2,1)S(1)} collective-permute-done((bf16[64,512]{1,0:T(8,128)(2,1)S(1)}, bf16[64,512]{1,0:T(8,128)(2,1)S(1)}, u32[]{:S(2)}, u32[]{:S(2)}) %collective-permute-start.1) | collective-permute-done | bytes 65568 | tf_op jit(solution)/shard_map/ppermute | solution.py:383
  18.3 0.9 %join.1 = (f32[2,64,256]{2,1,0:T(8,128)S(1)}, bf16[64,512]{1,0:T(8,128)(2,1)S(1)}) custom-call(s32[2]{0:T(128)S(1)} %pad_add_fusion.refs_0_, f32[2,64,256]{2,1,0:T(8,128)S(1)} %get-tuple-element.18.refs_1_.refs_9_, bf16[64,512]{1,0:T(8,128)(2,1)S(1)} %collective-permute-done.1.refs_2_.refs_11_, bf16[8,2,256,256]{3,2,1,0:T(8,128)(2,1)S(1)} %next_powers.1.refs_3_.refs_6_), custom_call_target="tpu_custom_call" | custom-call | flops 134217728 | tf_op jit(solution)/shard_map/join/pallas_call | solution.py:250
  19.2 2.8 %collective-permute-start.2 = (bf16[64,512]{1,0:T(8,128)(2,1)S(1)}, bf16[64,512]{1,0:T(8,128)(2,1)S(1)}, u32[]{:S(2)}, u32[]{:S(2)}) collective-permute-start(bf16[64,512]{1,0:T(8,128)(2,1)S(1)} %get-tuple-element.21), channel_id=1, source_target_pairs={{0,8},{4,12},{8,0},{12,4},{1,9},{5,13},{9,1},{13,5},{2,10},{6,14},... | collective-permute-start | bytes 196616 | tf_op jit(solution)/shard_map/ppermute | solution.py:383
  22.0 3.7 %collective-permute-done.2.refs_12_ = bf16[64,512]{1,0:T(8,128)(2,1)S(1)} collective-permute-done((bf16[64,512]{1,0:T(8,128)(2,1)S(1)}, bf16[64,512]{1,0:T(8,128)(2,1)S(1)}, u32[]{:S(2)}, u32[]{:S(2)}) %collective-permute-start.2) | collective-permute-done | bytes 65568 | tf_op jit(solution)/shard_map/ppermute | solution.py:383
  25.7 0.0 copy-done.6
  25.7 5.8 %down.1 = (f32[1024,256]{1,0:T(8,128)}, f32[1024,256]{1,0:T(8,128)}) custom-call(s32[2]{0:T(128)S(1)} %pad_add_fusion.refs_0_, f32[64,256]{1,0:T(8,128)S(1)} %copy-done.6, f32[1024,256]{1,0:T(8,128)S(1)} %get-tuple-element.14.refs_2_, f32[448,256]{1,0:T(8,128)S(1)} %get-tuple-element.15.refs_3_, f32[448,256]{1,0:T(8,128)S(1)} %get-tuple-element.16.refs_4_, ...), custom_call_target="tpu_custom_call" | custom-call | flops 1610612736 | tf_op jit(solution)/shard_map/down/pallas_call | solution.py:340
Async XLA Ops:
  0.6 1.6 %copy-start = (bf16[128,16,512]{2,1,0:T(8,128)(2,1)S(1)}, bf16[128,16,512]{2,1,0:T(8,128)(2,1)}, u32[]{:S(2)}) copy-start(bf16[128,16,512]{2,1,0:T(8,128)(2,1)} %refs_1_.5) | copy-start | bytes 6291460
  2.2 0.9 %copy-start.2 = (bf16[256,512]{1,0:T(8,128)(2,1)S(1)}, bf16[256,512]{1,0:T(8,128)(2,1)}, u32[]{:S(2)}) copy-start(bf16[256,512]{1,0:T(8,128)(2,1)} %refs_2_.4) | copy-start | bytes 786436
  3.2 2.2 %copy-start.1 = (bf16[128,16,512]{2,1,0:T(8,128)(2,1)S(1)}, bf16[128,16,512]{2,1,0:T(8,128)(2,1)}, u32[]{:S(2)}) copy-start(bf16[128,16,512]{2,1,0:T(8,128)(2,1)} %refs_1_.5) | copy-start | bytes 6291460
  3.2 2.2 %copy-start.3 = (bf16[256,512]{1,0:T(8,128)(2,1)S(1)}, bf16[256,512]{1,0:T(8,128)(2,1)}, u32[]{:S(2)}) copy-start(bf16[256,512]{1,0:T(8,128)(2,1)} %refs_2_.4) | copy-start | bytes 786436
  4.9 2.3 %copy-start.5 = (bf16[256,256]{1,0:T(8,128)(2,1)S(1)}, bf16[256,256]{1,0:T(8,128)(2,1)}, u32[]{:S(2)}) copy-start(bf16[256,256]{1,0:T(8,128)(2,1)} %refs_7_.1) | copy-start | bytes 393220
  4.9 5.9 %collective-permute-start = (bf16[1024,256]{1,0:T(8,128)(2,1)S(1)}, bf16[1024,256]{1,0:T(8,128)(2,1)S(1)}, u32[]{:S(2)}, u32[]{:S(2)}) collective-permute-start(bf16[1024,256]{1,0:T(8,128)(2,1)S(1)} %inputs_other.1), channel_id=1, source_target_pairs={{0,1},{1,0},{2,3},{3,2},{4,5},{5,4},{6,7},{7,6},{8,9},{9,8},{10,11... | collective-permute-start | bytes 1572872 | tf_op jit(solution)/shard_map/ppermute | solution.py:375
  5.4 1.8 %copy-start.4 = (f32[256,256]{1,0:T(8,128)S(1)}, f32[256,256]{1,0:T(8,128)}, u32[]{:S(2)}) copy-start(f32[256,256]{1,0:T(8,128)} %refs_8_.1) | copy-start | bytes 786436
  5.4 1.8 %copy-start.7 = (f32[256,256]{1,0:T(8,128)S(1)}, f32[256,256]{1,0:T(8,128)}, u32[]{:S(2)}) copy-start(f32[256,256]{1,0:T(8,128)} %refs_0_.1) | copy-start | bytes 786436
  12.9 5.4 %collective-permute-start.1 = (bf16[64,512]{1,0:T(8,128)(2,1)S(1)}, bf16[64,512]{1,0:T(8,128)(2,1)S(1)}, u32[]{:S(2)}, u32[]{:S(2)}) collective-permute-start(bf16[64,512]{1,0:T(8,128)(2,1)S(1)} %get-tuple-element.19), channel_id=1, source_target_pairs={{0,4},{4,0},{8,12},{12,8},{1,5},{5,1},{9,13},{13,9},{2,6},{6,2},{1... | collective-permute-start | bytes 196616 | tf_op jit(solution)/shard_map/ppermute | solution.py:383
  15.6 10.1 %copy-start.6 = (f32[64,256]{1,0:T(8,128)S(1)}, f32[64,256]{1,0:T(8,128)}, u32[]{:S(2)}) copy-start(f32[64,256]{1,0:T(8,128)} %refs_1_.7) | copy-start | bytes 196612
  19.2 6.5 %collective-permute-start.2 = (bf16[64,512]{1,0:T(8,128)(2,1)S(1)}, bf16[64,512]{1,0:T(8,128)(2,1)S(1)}, u32[]{:S(2)}, u32[]{:S(2)}) collective-permute-start(bf16[64,512]{1,0:T(8,128)(2,1)S(1)} %get-tuple-element.21), channel_id=1, source_target_pairs={{0,8},{4,12},{8,0},{12,4},{1,9},{5,13},{9,1},{13,5},{2,10},{6,14},... | collective-permute-start | bytes 196616 | tf_op jit(solution)/shard_map/ppermute | solution.py:383

commit v2 on v0

v2 whole, which is shorter than its diff:
```python
import jax
import jax.numpy as jnp
from jax import lax
from jax.experimental import pallas as pl
from jax.experimental.pallas import tpu as pltpu
from jax.sharding import PartitionSpec as P

F32 = jnp.float32
BF16 = jnp.bfloat16
LANES = 128
VMEM = pl.BlockSpec(memory_space=pltpu.VMEM)
SMEM = pl.BlockSpec(memory_space=pltpu.SMEM)
ANY = pl.BlockSpec(memory_space=pl.ANY)
PARAMS = pltpu.CompilerParams(vmem_limit_bytes=24 * 2**20)


def halves(x):
    high = x.astype(BF16)
    return high, (x - high.astype(F32)).astype(BF16)


def dot(x, y):
    return jnp.dot(x, y, preferred_element_type=F32)


def dot_nt(x, y):
    return lax.dot_general(x, y, (((1,), (1,)), ((), ())), preferred_element_type=F32)


def mul(x, y):
    return muls((x, y))


def muls(*terms):
    left, right = [], []
    for x, y in terms:
        left += [x[0], x[1], x[0]]
        right += [y[0], y[0], y[1]]
    return dot(jnp.concatenate(left, 1), jnp.concatenate(right, 0))


class Both:
    def __init__(self, first, second):
        self.stacks = first, second

    def of(self, name):
        return self.stacks[0] if name in self.stacks[0].place else self.stacks[1]

    def put(self, name, value):
        return self.of(name).put(name, value)

    def __getitem__(self, name):
        return self.of(name)[name]


class Stack:
    def __init__(self, names, ref):
        self.place = {name: i for i, name in enumerate(names)}
        self.ref = ref

    def put(self, name, value):
        pair = halves(value)
        self.copy(name, pair)
        return pair

    def copy(self, name, pair):
        self.ref[self.place[name], 0] = pair[0]
        self.ref[self.place[name], 1] = pair[1]

    def __getitem__(self, name):
        return self.ref[self.place[name], 0], self.ref[self.place[name], 1]


def stack_shape(names, n):
    return jax.ShapeDtypeStruct((len(names), 2, n, n), BF16)


def cost(flops):
    return pl.CostEstimate(flops=int(flops), bytes_accessed=0, transcendentals=0)


def split_cols(held, row, product):
    rows = product.shape[0]
    for j in range(held.shape[0]):
        held[j, pl.ds(row, rows)] = product[:, j * LANES : (j + 1) * LANES]


def by_step(held, out, members, steps):
    for t in range(steps):
        for j in range(held.shape[0]):
            step = held.at[j][pl.ds(t, members, stride=steps)]
            out[pl.ds(t * members, members), pl.ds(j * LANES, LANES)] = step.astype(out.dtype)


FIRST = ("a1", "a2", "a3", "a4", "g1", "g2", "g3", "g4", "w", "b")
SECOND = ("a8", "a12", "g8", "g12", "C0", "C1", "C2", "C3", "k4", "b1", "b2")
BLOCK = ("a", "g", "k", "c", "V0", "V1", "V2", "v0", "v1", "v2")
DOUBLE = ("a", "g", "k", "c")
READY = ("Z1x", "Z1d", "Z2d")


def first_powers(packed, transition):
    n = packed.shape[2]

    def kernel(packed, tr, out):
        m = Stack(FIRST, out)
        a1 = m.put("a1", packed[0].T)
        g_full = packed[1].T
        g1 = m.put("g1", g_full)
        w = m.put("w", dot(tr[...].T, g1[0]))
        a2, g2 = m.put("a2", mul(a1, a1)), m.put("g2", mul(g1, g1))
        m.put("b", g_full - mul(w, g1))
        m.put("a3", mul(a2, a1))
        m.put("a4", mul(a2, a2))
        m.put("g3", mul(g2, g1))
        m.put("g4", mul(g2, g2))

    return pl.pallas_call(
        kernel,
        out_shape=stack_shape(FIRST, n),
        in_specs=[VMEM, VMEM],
        out_specs=VMEM,
        compiler_params=PARAMS,
        cost_estimate=cost(1e9),
        name="first_powers",
    )(packed, transition)


def second_powers(first, own, other):
    n = first.shape[2]

    def kernel(first_ref, own, other, out, u, held, sem):
        copy = pltpu.make_async_copy(other, held, sem)
        copy.start()
        f, m = Stack(FIRST, first_ref), Stack(SECOND, out)
        a1, a2, a3, a4, g4, b = (f[name] for name in ("a1", "a2", "a3", "a4", "g4", "b"))
        full, beta = [b[0].astype(F32) + b[1].astype(F32)], [b]
        for i in range(1, 4):
            full.append(mul(b, f["g%d" % i]))
            beta.append(m.put(("b1", "b2", "C3")[i - 1], full[i]))
        a8, g8 = m.put("a8", mul(a4, a4)), m.put("g8", mul(g4, g4))
        c0 = m.put("C0", full[0] + muls((a1, beta[1]), (a2, beta[2]), (a3, beta[3])))
        m.put("C1", full[1] + muls((a1, beta[2]), (a2, beta[3])))
        m.put("C2", full[2] + mul(a1, beta[3]))
        m.put("a12", mul(a8, a4))
        m.put("g12", mul(g8, g4))
        m.put("k4", mul(a1, c0))
        copy.wait()
        u[...] = own[...] + held[...].astype(F32)

    return pl.pallas_call(
        kernel,
        out_shape=(stack_shape(SECOND, n), jax.ShapeDtypeStruct(own.shape, F32)),
        in_specs=[VMEM, VMEM, ANY],
        out_specs=(VMEM, VMEM),
        scratch_shapes=[pltpu.VMEM(other.shape, BF16), pltpu.SemaphoreType.DMA],
        compiler_params=PARAMS,
        cost_estimate=cost(1.5e9),
        name="second_powers",
    )(first, own, other)


def half_inputs(place, obs, gain, members, sign, dtype):
    steps, sensors = obs.shape[1:]
    states = gain.shape[0]
    cut = 16
    rows = cut * steps

    def kernel(place, obs, gain, out, held):
        half = place[0] if sign > 0 else 1 - place[0]
        for i in range(members // cut):
            part = obs[pl.ds(half * members + i * cut, cut)].reshape(rows, sensors)
            split_cols(held, i * rows, dot_nt(part, gain[...]))
        by_step(held, out, members, steps)

    return pl.pallas_call(
        kernel,
        out_shape=jax.ShapeDtypeStruct((members * steps, states), dtype),
        in_specs=[SMEM, VMEM, VMEM],
        out_specs=VMEM,
        scratch_shapes=[pltpu.VMEM((states // LANES, members * steps, LANES), F32)],
        compiler_params=PARAMS,
        cost_estimate=cost(2 * rows * sensors * states * 4),
        name="inputs_own" if sign > 0 else "inputs_other",
    )(place, obs, gain)


def put_payload(payload, e, h):
    states = e.shape[1]
    payload[:, pl.ds(0, states)] = e.astype(BF16)
    payload[:, pl.ds(states, states)] = h.astype(BF16)


def up(u, first, second, members):
    rows, states = u.shape
    quads = rows // members // 4

    def kernel(u, first_ref, second_ref, e_out, x_out, d_out, ends, payload):
        f = s = Both(Stack(FIRST, first_ref), Stack(SECOND, second_ref))
        u = u[...].reshape(quads, 4, members, states)
        full = [u[:, j].reshape(-1, states) for j in range(4)]
        pairs = [halves(x) for x in full]
        e = full[3] + muls((pairs[2], f["a1"]), (pairs[1], f["a2"]), (pairs[0], f["a3"]))
        h = muls(*((pairs[j], s["C%d" % j]) for j in range(4)))
        e_out[...] = e
        cut = lambda x, q: x[q * members : (q + 1) * members]
        ah = [f["a4"], s["a8"], s["a12"]]
        gh = [f["g4"], s["g8"], s["g12"]]
        ep = [halves(cut(e, q)) for q in range(quads)]
        entering = [cut(e, 0)]
        for q in range(1, quads):
            entering.append(cut(e, q) + muls(*((ep[p], ah[q - p - 1]) for p in range(q))))
        x = jnp.concatenate(entering[:-1], 0)
        x_out[...] = x
        back_x = mul(halves(x), s["k4"])
        backs = [cut(h, 0)] + [cut(h, q) + cut(back_x, q - 1) for q in range(1, quads)]
        bp = [halves(x) for x in backs]
        handed = [
            backs[q] + muls(*((bp[p], gh[p - q - 1]) for p in range(q + 1, quads))) for q in range(quads - 1)
        ] + [backs[-1]]
        d_out[...] = jnp.concatenate(handed[1:], 0)
        ends[0] = entering[-1]
        ends[1] = handed[0]
        put_payload(payload, entering[-1], handed[0])

    return pl.pallas_call(
        kernel,
        out_shape=(
            jax.ShapeDtypeStruct((quads * members, states), F32),
            jax.ShapeDtypeStruct(((quads - 1) * members, states), F32),
            jax.ShapeDtypeStruct(((quads - 1) * members, states), F32),
            jax.ShapeDtypeStruct((2, members, states), F32),
            jax.ShapeDtypeStruct((members, 2 * states), BF16),
        ),
        in_specs=[VMEM] * 3,
        out_specs=(VMEM,) * 5,
        compiler_params=PARAMS,
        cost_estimate=cost(2e9),
        name="up",
    )(u, first, second)


def block_maps(mats_in, single, after):
    n = mats_in.shape[2]

    def kernel(mats_ref, single_ref, _, out):
        f = s = Both(Stack(FIRST, mats_ref), Stack(SECOND, single_ref))
        mats = Stack(BLOCK, out)
        k4, a4, g4, a8, g8 = s["k4"], f["a4"], f["g4"], s["a8"], s["g8"]
        full = [mul(x, k4) for x in (a4, a8, s["a12"])]
        t = [halves(x) for x in full]
        mats.put("a", mul(a8, a8))
        g = mats.put("g", mul(g8, g8))
        k = k4[0].astype(F32) + k4[1].astype(F32)
        k = mats.put("k", k + muls((t[0], g4), (t[1], g8), (t[2], s["g12"])))
        mats.put("V0", full[0] + muls((t[1], g4), (t[2], g8)))
        mats.put("V1", full[1] + mul(t[2], g4))
        mats.copy("V2", t[2])
        mats.put("c", mul(k, g))
        b, b1, b2, a2, a3 = f["b"], f["b1"], f["b2"], f["a2"], f["a3"]
        mats.put("v2", mul(a4, b))
        mats.put("v1", muls((a3, b), (a4, b1)))
        mats.put("v0", muls((a2, b), (a3, b1), (a4, b2)))

    return pl.pallas_call(
        kernel,
        out_shape=stack_shape(BLOCK, n),
        in_specs=[VMEM, VMEM, ANY],
        out_specs=VMEM,
        compiler_params=PARAMS,
        cost_estimate=cost(1.2e9),
        name="block_maps",
    )(mats_in, single, after)


def double_maps(names, given, last):
    n = given.shape[2]
    kept = DOUBLE[:3] if last else DOUBLE

    def kernel(given_ref, out):
        s = Stack(names, given_ref)
        mats = Stack(kept, out)
        a, g, k = s["a"], s["g"], s["k"]
        mats.put("a", mul(a, a))
        g = mats.put("g", mul(g, g))
        k = mats.put("k", k[0].astype(F32) + k[1].astype(F32) + mul(a, s["c"]))
        if not last:
            mats.put("c", mul(k, g))

    return pl.pallas_call(
        kernel,
        out_shape=stack_shape(kept, n),
        in_specs=[VMEM],
        out_specs=VMEM,
        compiler_params=PARAMS,
        cost_estimate=cost(4e8),
        name="double_maps",
    )(given)


def sides(bit, mine, got):
    states = mine.shape[2]
    got_e = got[:, pl.ds(0, states)].astype(F32)
    got_h = got[:, pl.ds(states, states)].astype(F32)
    right = bit > 0
    el, er = jnp.where(right, got_e, mine[0]), jnp.where(right, mine[0], got_e)
    hl, hr = jnp.where(right, got_h, mine[1]), jnp.where(right, mine[1], got_h)
    return el, er, hl, hr


def join(level, names, bits, mine, got, mats):
    def kernel(bits, mine, got, mats_ref, ends, payload):
        m = Stack(names, mats_ref)
        el, er, hl, hr = sides(bits[level], mine, got)
        pair = halves(el)
        e = mul(pair, m["a"]) + er
        h = hl + muls((halves(hr), m["g"]), (pair, m["c"]))
        ends[0] = e
        ends[1] = h
        put_payload(payload, e, h)

    return pl.pallas_call(
        kernel,
        out_shape=(jax.ShapeDtypeStruct(mine.shape, F32), jax.ShapeDtypeStruct(got.shape, BF16)),
        in_specs=[SMEM, VMEM, VMEM, VMEM],
        out_specs=(VMEM, VMEM),
        compiler_params=PARAMS,
        cost_estimate=cost(1e8),
        name="join",
    )(bits, mine, got, mats)


def either(flag, x, y):
    return tuple(jnp.where(flag, p, q) for p, q in zip(x, y, strict=True))


def ready(bits, begin, u, e_groups, mats_in, single, maps, ends, got):
    members, states = begin.shape
    rows = u.shape[0]
    quads = rows // members // 4
    top = len(maps) - 1

    def kernel(bits, begin, u, e_groups, mats_ref, single_ref, *refs):
        f = Both(Stack(FIRST, mats_ref), Stack(SECOND, single_ref))
        level_maps = [Stack(BLOCK if i == 0 else DOUBLE, refs[i]) for i in range(top + 1)]
        mine = refs[top + 1 : 2 * top + 2]
        arrived = refs[2 * top + 2 : 3 * top + 2]
        out_ref, pre, local, local_d = refs[3 * top + 2 :]
        mats = Stack(READY, out_ref)
        unit = halves(jnp.eye(states, dtype=F32))
        none = tuple(jnp.zeros_like(x) for x in unit)
        zero = jnp.zeros((members, states), F32)
        p, q, r, px, pd = unit, unit, none, zero, zero
        for i in range(top):
            m = level_maps[i]
            right = bits[i] > 0
            el, _, _, hr = sides(bits[i], mine[i], arrived[i])
            elp = halves(el)
            hand = mul(elp, m["k"]) + hr
            ak = halves(mul(m["a"], m["k"]))
            if i == 0:
                p, q, r = either(right, m["a"], unit), either(right, unit, m["g"]), either(right, none, ak)
                px, pd = jnp.where(right, el, zero), jnp.where(right, zero, hand)
            else:
                px, pd = (
                    jnp.where(right, mul(elp, p) + px, px),
                    jnp.where(right, mul(elp, r) + pd, mul(halves(hand), q) + pd),
                )
                r = either(
                    right,
                    halves(mul(m["a"], r)),
                    halves(mul(ak, q) + r[0].astype(F32) + r[1].astype(F32)),
                )
                p, q = either(right, halves(mul(m["a"], p)), p), either(right, q, halves(mul(m["g"], q)))
        m = level_maps[top]
        right = bits[top] > 0
        w = f["w"]
        x0 = begin[...]
        own_e = mine[top][0]
        aw = halves(mul(m["a"], w))
        wg = halves(mul(w, m["g"]))
        middle = mul(halves(x0), m["a"]) + jnp.where(right, zero, own_e)
        middle_p = halves(middle)
        far = halves(mul(aw, m["g"]) + m["k"][0].astype(F32) + m["k"][1].astype(F32))
        x_in = jnp.where(right, middle, x0)
        d_in = mul(middle_p, either(right, aw, far)) + jnp.where(right, mul(halves(own_e), w), zero)
        x_in_p = halves(x_in)
        pre[0] = mul(x_in_p, p) + px
        pre[1] = muls((halves(d_in), q), (x_in_p, r)) + pd
        mats.copy("Z1x", either(right, p, none))
        after = mul(either(right, aw, wg), q)
        after_r = r[0].astype(F32) + r[1].astype(F32)
        mats.put("Z1d", jnp.where(right, after + after_r, after))
        mats.copy("Z2d", either(right, none, q))
        b, b1, b2 = f["b"], f["b1"], f["b2"]
        v = u[...].reshape(quads, 4, members, states)
        part = [v[:, j].reshape(-1, states) for j in range(3)]
        pairs = [halves(x) for x in part[:2]]
        f1 = part[1] + mul(pairs[0], f["a1"])
        f2 = part[2] + muls((pairs[1], f["a1"]), (pairs[0], f["a2"]))
        local[0], local[1], local[2], local[3] = part[0], f1, f2, e_groups[...]
        p1, p2, p3 = halves(f1), halves(f2), halves(e_groups[...])
        local_d[2] = mul(p3, b)
        local_d[1] = muls((p2, b), (p3, b1))
        local_d[0] = muls((p1, b), (p2, b1), (p3, b2))

    return pl.pallas_call(
        kernel,
        out_shape=(
            stack_shape(READY, states),
            jax.ShapeDtypeStruct((2, members, states), F32),
            jax.ShapeDtypeStruct((4, quads * members, states), F32),
            jax.ShapeDtypeStruct((3, quads * members, states), F32),
        ),
        in_specs=[SMEM] + [VMEM] * (5 + len(maps) + len(ends) + len(got)),
        out_specs=(VMEM,) * 4,
        compiler_params=PARAMS,
        cost_estimate=cost(3e9),
        name="ready",
    )(bits, begin, u, e_groups, mats_in, single, *maps, *ends, *got)


def finish(bits, got, prepared, pre, local, local_d, x_groups, d_groups, mats, single, block, transition, gain):
    members, states = pre.shape[1:]
    quads = local.shape[1] // members
    steps = 4 * quads
    groups = bits.shape[0]

    def kernel(bits, got, ready_ref, pre, local, local_d, xg, dg, mats_ref, single_ref, block_ref, tr, ga, *refs):
        filtered, smoothed, filtered_held, smoothed_held, sems = refs
        z, m = Stack(READY, ready_ref), Stack(BLOCK, block_ref)
        f = s = Both(Stack(FIRST, mats_ref), Stack(SECOND, single_ref))
        e, h = got[:, pl.ds(0, states)], got[:, pl.ds(states, states)]
        exact = lambda x, y: dot(x, y[0]) + dot(x, y[1])
        x = exact(e, z["Z1x"]) + pre[0]
        d = exact(e, z["Z1d"]) + exact(h, z["Z2d"]) + pre[1]
        xp, dp = halves(x), halves(d)
        ah, gh = [f["a4"], s["a8"], s["a12"]], [f["g4"], s["g8"], s["g12"]]
        xs, ds = [x], []
        for q in range(1, quads):
            part = pl.ds((q - 1) * members, members)
            xs.append(xg[part] + mul(xp, ah[q - 1]))
            ds.append(dg[part] + muls((dp, gh[quads - q - 1]), (xp, m["V%d" % (q - 1)])))
        x = jnp.concatenate(xs, 0)
        d = jnp.concatenate(ds + [d], 0)
        xp, dp = halves(x), halves(d)
        low = ga[...].astype(BF16)
        final = bits[0] > 0
        for i in range(1, groups):
            final = jnp.logical_and(final, bits[i] > 0)

        def write(held, j, value):
            for q in range(quads):
                for c in range(held.shape[0]):
                    piece = value[q * members : (q + 1) * members, c * LANES : (c + 1) * LANES]
                    held.at[c][pl.ds(4 * q + j, members, stride=steps)] = piece

        def send(held, out, sem):
            copies = []
            for c in range(held.shape[0]):
                copies.append(pltpu.make_async_copy(held.at[c], out.at[:, pl.ds(c * LANES, LANES)], sem.at[c]))
                copies[-1].start()
            return copies

        states_of = []
        for j in range(4):
            value = local[j] + mul(xp, f["a%d" % (j + 1)])
            states_of.append(value)
            write(filtered_held, j, value)
        copies = send(filtered_held, filtered, sems.at[0])
        for j in range(4):
            value = states_of[j]
            if j < 3:
                handed = local_d[j] + muls((dp, f["g%d" % (3 - j)]), (xp, m["v%d" % j]))
            else:
                handed = d
            predicted = dot_nt(value.astype(BF16), tr[...]).astype(BF16)
            result = value - dot_nt(predicted, low) + handed
            if j == 3:
                tail = (quads - 1) * members
                result = jnp.concatenate([result[:tail], jnp.where(final, value[tail:], result[tail:])], 0)
            write(smoothed_held, j, result)
        copies += send(smoothed_held, smoothed, sems.at[1])
        for copy in copies:
            copy.wait()

    return pl.pallas_call(
        kernel,
        out_shape=(jax.ShapeDtypeStruct((members * steps, states), F32),) * 2,
        in_specs=[SMEM] + [VMEM] * 12,
        out_specs=(ANY,) * 2,
        scratch_shapes=[
            pltpu.VMEM((states // LANES, members * steps, LANES), F32),
            pltpu.VMEM((states // LANES, members * steps, LANES), F32),
            pltpu.SemaphoreType.DMA((2, states // LANES)),
        ],
        compiler_params=PARAMS,
        cost_estimate=cost(3e9),
        name="finish",
    )(bits, got, prepared, pre, local, local_d, x_groups, d_groups, mats, single, block, transition, gain)


def body(observations, obs_gain, closed_loop, transition, smoother_gain, initial_mean):
    members, states = initial_mean.shape
    steps = observations.shape[1]
    assert steps == 16
    blocks = lax.axis_size("tm")
    groups = blocks.bit_length() - 1
    assert blocks == 1 << groups
    place = lax.axis_index("sens").astype(jnp.int32).reshape(1)
    position = lax.axis_index("tm").astype(jnp.int32)
    bits = jnp.stack([(position >> i) & 1 for i in range(groups)])

    packed = jnp.stack([closed_loop, smoother_gain])
    to_send = half_inputs(place, observations, obs_gain, members, -1, BF16)
    other = lax.ppermute(to_send, "sens", [(0, 1), (1, 0)])
    own = half_inputs(place, observations, obs_gain, members, 1, F32)
    mats = first_powers(packed, transition)
    single, u = second_powers(mats, own, other)
    e_groups, x_groups, d_groups, ends, payload = up(u, mats, single, members)
    block = block_maps(mats, single, ends)
    maps = [block]
    for i in range(1, groups):
        maps.append(double_maps(BLOCK if i == 1 else DOUBLE, maps[-1], i == groups - 1))
    mine, got = [ends], []
    for i in range(groups):
        arrived = lax.ppermute(payload, "tm", [(j, j ^ (1 << i)) for j in range(blocks)])
        got.append(arrived)
        if i < groups - 1:
            ends, payload = join(i, BLOCK if i == 0 else DOUBLE, bits, ends, arrived, maps[i])
            mine.append(ends)
    prepared, pre, local, local_d = ready(
        bits, initial_mean, u, e_groups, mats, single, maps, mine, got[:-1]
    )
    filtered, smoothed = finish(
        bits, got[-1], prepared, pre, local, local_d, x_groups, d_groups, mats, single, block, transition, smoother_gain
    )
    shape = (members, steps, states)
    return filtered.reshape(shape), smoothed.reshape(shape)


def solution(mesh):
    placed = (
        P(("rec", "state"), "tm", "sens"),
        P(None, "sens"),
        P(),
        P(),
        P(),
        P(("rec", "state", "sens"), None),
    )
    return jax.shard_map(
        body,
        mesh=mesh,
        in_specs=placed,
        out_specs=(
            P(("rec", "state", "sens"), "tm", None),
            P(("rec", "state", "sens"), "tm", None),
        ),
        check_vma=False,
    )
```

time: 167 us -> 27.8 us (0.17); the launches traced: 164 us -> 27.6 us
  matrix products: 89.8 us -> 0 us
  blocking collectives: 29.4 us -> 0 us
  Pallas kernels: 0 us -> 17.5 us
  local copies, waits for them, and re-layouts: 18.1 us -> 2.85 us
  between operations: 15.7 us -> 0.78 us
  starting transfers between devices: 0.13 us -> 6.34 us
  waiting for transfers between devices: 6.21 us -> 0.01 us
  loops' own time: 2.32 us -> 0 us
  other arithmetic: 2.11 us -> 0.11 us
    dot_general x81 -> x0, matrix products: 89.8 us -> none  [the longest x79 82.9 us: product(): jnp.dot(left, right, precision=lax.Precision.HIGHEST, preferred_element_t...]
    all_gather x2 -> x0, blocking collectives: 29.4 us -> none  [prefix_2(): everything = jax.tree.map(lambda part: lax.all_gather(part, axis), array)]
    pallas_call x0 -> x10, Pallas kernels: none -> 17.5 us  [the longest x1 4.94 us: finish(): pl.pallas_call(kernel, out_shape=(jax.ShapeDtypeStruct((members * steps,...]
    dynamic_update_slice x30 -> x0, local copies, waits for them, and re-layouts: 14.4 us -> none  [body(): _, earlier = lax.scan(backward, closing, adjusted[:-1], reverse=True)]
    ppermute x0 -> x3, starting transfers between devices: none -> 6.34 us  [the longest x2 5.82 us: body(): lax.ppermute(payload, 'tm', [(j, j ^ 1 << i) for j in range(blocks)])]
    reduce_scatter x1 -> x0, waiting for transfers between devices: 6.16 us -> none  [body(): lax.psum_scatter(jnp.einsum('bts,ks->btk', observations, obs_gain, prefer...]
    another operation x6 -> x0, loops' own time: 2.32 us -> none  [the longest x1 0.69 us: body(): _, earlier = lax.scan(backward, closing, adjusted[:-1], reverse=True)]
    transpose x1 -> x0, other arithmetic: 2.02 us -> none  [body(): return (jnp.swapaxes(filtered, 0, 1), jnp.swapaxes(smoothed, 0, 1))]
  transfers between devices with their start and end apart: 3 -> 3, of which waited for: 1 -> 0; matrix products, arithmetic and copies ran while one was open for 39% -> 0% of each run, Pallas kernels for 0% -> 26%
where the time goes in v2:
time: 27.8 us; the launch traced here: 27.6 us
  Pallas kernels  17.5 us (63%)
  starting transfers between devices  6.34 us (23%)
  local copies, waits for them, and re-layouts  2.85 us (10%)
  between operations  0.78 us (3%)
    ppermute x2, starting transfers between devices, body(): lax.ppermute(payload, 'tm', [(j, j ^ 1 << i) for j in range(blocks)])  5.82 us
    pallas_call x1, Pallas kernels, finish(): pl.pallas_call(kernel, out_shape=(jax.ShapeDtypeStruct((members * steps,...  4.94 us
    unnamed x16, local copies, waits for them, and re-layouts  2.85 us
    pallas_call x1, Pallas kernels, ready(): pl.pallas_call(kernel, out_shape=(stack_shape(READY, states), jax.ShapeDt...  2.83 us
    pallas_call x1, Pallas kernels, block_maps(): pl.pallas_call(kernel, out_shape=stack_shape(BLOCK, n), in_specs=[VMEM, V...  2.11 us
    pallas_call x1, Pallas kernels, up(): pl.pallas_call(kernel, out_shape=(jax.ShapeDtypeStruct((quads * members,...  1.88 us
    pallas_call x1, Pallas kernels, second_powers(): pl.pallas_call(kernel, out_shape=(stack_shape(SECOND, n), jax.ShapeDtypeS...  1.81 us
    pallas_call x2, Pallas kernels, half_inputs(): pl.pallas_call(kernel, out_shape=jax.ShapeDtypeStruct((members * steps, s...  1.45 us
  transfers between devices with their start and end apart: 3, of which 0 were waited for; matrix products, arithmetic and copies ran while one was open for 0% of the time, Pallas kernels for 26%

profile of v2, /device:TPU:0, one launch (start us, length us, event | category | flops | bytes accessed | tf_op | source)
XLA Modules:
  0.0 27.6 jit_solution(391273428151564225)
XLA Ops:
  0.6 0.0 copy-start
  0.6 1.6 %copy-done = bf16[128,16,512]{2,1,0:T(8,128)(2,1)S(1)} copy-done((bf16[128,16,512]{2,1,0:T(8,128)(2,1)S(1)}, bf16[128,16,512]{2,1,0:T(8,128)(2,1)}, u32[]{:S(2)}) %copy-start) | copy-done | bytes 2097176
  2.2 0.0 copy-start.2
  2.2 0.9 %copy-done.2 = bf16[256,512]{1,0:T(8,128)(2,1)S(1)} copy-done((bf16[256,512]{1,0:T(8,128)(2,1)S(1)}, bf16[256,512]{1,0:T(8,128)(2,1)}, u32[]{:S(2)}) %copy-start.2) | copy-done | bytes 262168
  3.2 0.0 copy-start.1
  3.2 0.0 copy-start.3
  3.2 0.0 copy-start.4
  3.2 0.0 copy-start.7
  3.2 0.7 %inputs_other.1 = bf16[1024,256]{1,0:T(8,128)(2,1)S(1)} custom-call(s32[1]{0:T(128)} %bitcast.4.place, bf16[128,16,512]{2,1,0:T(8,128)(2,1)S(1)} %copy-done, bf16[256,512]{1,0:T(8,128)(2,1)S(1)} %copy-done.2), custom_call_target="tpu_custom_call" | custom-call | flops 268435456 | tf_op jit(solution)/shard_map/inputs_other/pallas_call | solution.py:176
  3.9 0.0 copy-start.5
  4.0 0.5 %collective-permute-start = (bf16[1024,256]{1,0:T(8,128)(2,1)S(1)}, bf16[1024,256]{1,0:T(8,128)(2,1)}, u32[]{:S(2)}, u32[]{:S(2)}) collective-permute-start(bf16[1024,256]{1,0:T(8,128)(2,1)S(1)} %inputs_other.1), channel_id=1, source_target_pairs={{0,1},{1,0},{2,3},{3,2},{4,5},{5,4},{6,7},{7,6},{8,9},{9,8},{10,11... | collective-permute-start | bytes 1572872 | tf_op jit(solution)/shard_map/ppermute | solution.py:516
  4.5 0.3 %copy-done.1 = bf16[128,16,512]{2,1,0:T(8,128)(2,1)S(1)} copy-done((bf16[128,16,512]{2,1,0:T(8,128)(2,1)S(1)}, bf16[128,16,512]{2,1,0:T(8,128)(2,1)}, u32[]{:S(2)}) %copy-start.1) | copy-done | bytes 2097176
  4.8 0.0 copy-done.3
  4.8 0.7 %inputs_own.1.own = f32[1024,256]{1,0:T(8,128)S(1)} custom-call(s32[1]{0:T(128)} %bitcast.4.place, bf16[128,16,512]{2,1,0:T(8,128)(2,1)S(1)} %copy-done.1, bf16[256,512]{1,0:T(8,128)(2,1)S(1)} %copy-done.3), custom_call_target="tpu_custom_call" | custom-call | flops 268435456 | tf_op jit(solution)/shard_map/inputs_own/pallas_call | solution.py:176
  5.5 0.0 copy-done.4
  5.5 0.0 copy-done.7
  5.5 0.0 copy-done.5
  5.6 1.1 %first_powers.1.first_ref.mats_ref = bf16[10,2,256,256]{3,2,1,0:T(8,128)(2,1)S(1)} custom-call(f32[2,256,256]{2,1,0:T(8,128)S(1)} %pad_maximum_fusion.packed, bf16[256,256]{1,0:T(8,128)(2,1)S(1)} %copy-done.5), custom_call_target="tpu_custom_call" | custom-call | flops 1000000000 | tf_op jit(solution)/shard_map/first_powers/pallas_call | solution.py:118
  6.7 0.1 pad_add_fusion.bits
  6.7 0.0 collective-permute-done.other
  6.7 1.8 %second_powers.1 = (bf16[11,2,256,256]{3,2,1,0:T(8,128)(2,1)S(1)}, f32[1024,256]{1,0:T(8,128)S(1)}) custom-call(bf16[10,2,256,256]{3,2,1,0:T(8,128)(2,1)S(1)} %first_powers.1.first_ref.mats_ref, f32[1024,256]{1,0:T(8,128)S(1)} %inputs_own.1.own, bf16[1024,256]{1,0:T(8,128)(2,1)} %collective-permute-done.other), custom_call_target="tpu_custom_call" | custom-call | flops 1500000000 | tf_op jit(solution)/shard_map/second_powers/pallas_call | solution.py:151
  8.6 1.9 %up.1 = (f32[256,256]{1,0:T(8,128)S(1)}, f32[192,256]{1,0:T(8,128)S(1)}, f32[192,256]{1,0:T(8,128)S(1)}, f32[2,64,256]{2,1,0:T(8,128)S(1)}, bf16[64,512]{1,0:T(8,128)(2,1)S(1)}) custom-call(f32[1024,256]{1,0:T(8,128)S(1)} %get-tuple-element.17.u, bf16[10,2,256,256]{3,2,1,0:T(8,128)(2,1)S(1)} %first_powers.1.first_ref.mats_ref, ...), custom_call_target="tpu_custom_call" | custom-call | flops 2000000000 | tf_op jit(solution)/shard_map/up/pallas_call | solution.py:226
  10.4 3.1 %collective-permute-start.1 = (bf16[64,512]{1,0:T(8,128)(2,1)S(1)}, bf16[64,512]{1,0:T(8,128)(2,1)S(1)}, u32[]{:S(2)}, u32[]{:S(2)}) collective-permute-start(bf16[64,512]{1,0:T(8,128)(2,1)S(1)} %get-tuple-element.20), channel_id=1, source_target_pairs={{0,4},{4,0},{8,12},{12,8},{1,5},{5,1},{9,13},{13,9},{2,6},{6,2},{1... | collective-permute-start | bytes 196616 | tf_op jit(solution)/shard_map/ppermute | solution.py:527
  13.5 2.1 %block_maps.1.mats_ref.given_ref.refs_0_.block_ref = bf16[10,2,256,256]{3,2,1,0:T(8,128)(2,1)S(1)} custom-call(bf16[10,2,256,256]{3,2,1,0:T(8,128)(2,1)S(1)} %first_powers.1.first_ref.mats_ref, bf16[11,2,256,256]{3,2,1,0:T(8,128)(2,1)S(1)} %get-tuple-element.18.second_ref.single_ref, f32[2,64,256]{2,1,0:T(8,128)S(1)} %get-tuple-element.19._.mine.refs_2_), custom_call_target="tpu_custom_call" | custom-call | flops 1200000000 | tf_op jit(solution)/shard_map/block_maps/pallas_call | solution.py:265
  15.6 0.0 copy-start.6
  15.7 0.5 %double_maps.1.refs_1_ = bf16[3,2,256,256]{3,2,1,0:T(8,128)(2,1)S(1)} custom-call(bf16[10,2,256,256]{3,2,1,0:T(8,128)(2,1)S(1)} %block_maps.1.mats_ref.given_ref.refs_0_.block_ref), custom_call_target="tpu_custom_call" | custom-call | flops 400000000 | tf_op jit(solution)/shard_map/double_maps/pallas_call | solution.py:290
  16.2 0.0 collective-permute-done.1.got.refs_4_
  16.2 0.9 %join.1 = (f32[2,64,256]{2,1,0:T(8,128)S(1)}, bf16[64,512]{1,0:T(8,128)(2,1)S(1)}) custom-call(s32[2]{0:T(128)S(1)} %pad_add_fusion.bits, f32[2,64,256]{2,1,0:T(8,128)S(1)} %get-tuple-element.19._.mine.refs_2_, bf16[64,512]{1,0:T(8,128)(2,1)S(1)} %collective-permute-done.1.got.refs_4_, ...), custom_call_target="tpu_custom_call" | custom-call | flops 100000000 | tf_op jit(solution)/shard_map/join/pallas_call | solution.py:322
  17.0 2.7 %collective-permute-start.2 = (bf16[64,512]{1,0:T(8,128)(2,1)S(1)}, bf16[64,512]{1,0:T(8,128)(2,1)S(1)}, u32[]{:S(2)}, u32[]{:S(2)}) collective-permute-start(bf16[64,512]{1,0:T(8,128)(2,1)S(1)} %get-tuple-element.21), channel_id=1, source_target_pairs={{0,8},{4,12},{8,0},{12,4},{1,9},{5,13},{9,1},{13,5},{2,10},{6,14},... | collective-permute-start | bytes 196616 | tf_op jit(solution)/shard_map/ppermute | solution.py:527
  19.8 0.0 copy-done.6
  19.8 2.8 %ready.1 = (bf16[3,2,256,256]{3,2,1,0:T(8,128)(2,1)S(1)}, f32[2,64,256]{2,1,0:T(8,128)S(1)}, f32[4,256,256]{2,1,0:T(8,128)S(1)}, f32[3,256,256]{2,1,0:T(8,128)S(1)}) custom-call(s32[2]{0:T(128)S(1)} %pad_add_fusion.bits, f32[64,256]{1,0:T(8,128)S(1)} %copy-done.6, f32[1024,256]{1,0:T(8,128)S(1)} %get-tuple-element.17.u, ...), custom_call_target="tpu_custom_call" | custom-call | flops 3000000000 | tf_op jit(solution)/shard_map/ready/pallas_call | solution.py:407
  22.6 0.0 collective-permute-done.2.got
  22.6 4.9 %finish.1 = (f32[1024,256]{1,0:T(8,128)}, f32[1024,256]{1,0:T(8,128)}) custom-call(s32[2]{0:T(128)S(1)} %pad_add_fusion.bits, bf16[64,512]{1,0:T(8,128)(2,1)S(1)} %collective-permute-done.2.got, bf16[3,2,256,256]{3,2,1,0:T(8,128)(2,1)S(1)} %get-tuple-element.24.ready_ref, f32[2,64,256]{2,1,0:T(8,128)S(1)} %get-tuple-element.25.pre, ...), custom_call_target="tpu_custom_call" | custom-call | flops 3000000000 | tf_op jit(solution)/shard_map/finish/pallas_call | solution.py:487
  (1 shorter events, 0.0 us)
Async XLA Ops:
  0.6 1.6 %copy-start = (bf16[128,16,512]{2,1,0:T(8,128)(2,1)S(1)}, bf16[128,16,512]{2,1,0:T(8,128)(2,1)}, u32[]{:S(2)}) copy-start(bf16[128,16,512]{2,1,0:T(8,128)(2,1)} %obs.3) | copy-start | bytes 6291460
  2.2 0.9 %copy-start.2 = (bf16[256,512]{1,0:T(8,128)(2,1)S(1)}, bf16[256,512]{1,0:T(8,128)(2,1)}, u32[]{:S(2)}) copy-start(bf16[256,512]{1,0:T(8,128)(2,1)} %gain.3) | copy-start | bytes 786436
  3.2 1.6 %copy-start.1 = (bf16[128,16,512]{2,1,0:T(8,128)(2,1)S(1)}, bf16[128,16,512]{2,1,0:T(8,128)(2,1)}, u32[]{:S(2)}) copy-start(bf16[128,16,512]{2,1,0:T(8,128)(2,1)} %obs.3) | copy-start | bytes 6291460
  3.2 1.6 %copy-start.3 = (bf16[256,512]{1,0:T(8,128)(2,1)S(1)}, bf16[256,512]{1,0:T(8,128)(2,1)}, u32[]{:S(2)}) copy-start(bf16[256,512]{1,0:T(8,128)(2,1)} %gain.3) | copy-start | bytes 786436
  3.2 2.3 %copy-start.4 = (f32[256,256]{1,0:T(8,128)S(1)}, f32[256,256]{1,0:T(8,128)}, u32[]{:S(2)}) copy-start(f32[256,256]{1,0:T(8,128)} %ga.1) | copy-start | bytes 786436
  3.2 2.3 %copy-start.7 = (f32[256,256]{1,0:T(8,128)S(1)}, f32[256,256]{1,0:T(8,128)}, u32[]{:S(2)}) copy-start(f32[256,256]{1,0:T(8,128)} %param.8) | copy-start | bytes 786436
  3.9 1.6 %copy-start.5 = (bf16[256,256]{1,0:T(8,128)(2,1)S(1)}, bf16[256,256]{1,0:T(8,128)(2,1)}, u32[]{:S(2)}) copy-start(bf16[256,256]{1,0:T(8,128)(2,1)} %tr.3) | copy-start | bytes 393220
  4.0 2.8 %collective-permute-start = (bf16[1024,256]{1,0:T(8,128)(2,1)S(1)}, bf16[1024,256]{1,0:T(8,128)(2,1)}, u32[]{:S(2)}, u32[]{:S(2)}) collective-permute-start(bf16[1024,256]{1,0:T(8,128)(2,1)S(1)} %inputs_other.1), channel_id=1, source_target_pairs={{0,1},{1,0},{2,3},{3,2},{4,5},{5,4},{6,7},{7,6},{8,9},{9,8},{10,11... | collective-permute-start | bytes 1572872 | tf_op jit(solution)/shard_map/ppermute | solution.py:516
  10.4 5.7 %collective-permute-start.1 = (bf16[64,512]{1,0:T(8,128)(2,1)S(1)}, bf16[64,512]{1,0:T(8,128)(2,1)S(1)}, u32[]{:S(2)}, u32[]{:S(2)}) collective-permute-start(bf16[64,512]{1,0:T(8,128)(2,1)S(1)} %get-tuple-element.20), channel_id=1, source_target_pairs={{0,4},{4,0},{8,12},{12,8},{1,5},{5,1},{9,13},{13,9},{2,6},{6,2},{1... | collective-permute-start | bytes 196616 | tf_op jit(solution)/shard_map/ppermute | solution.py:527
  15.6 4.1 %copy-start.6 = (f32[64,256]{1,0:T(8,128)S(1)}, f32[64,256]{1,0:T(8,128)}, u32[]{:S(2)}) copy-start(f32[64,256]{1,0:T(8,128)} %begin.1) | copy-start | bytes 196612
  17.0 5.6 %collective-permute-start.2 = (bf16[64,512]{1,0:T(8,128)(2,1)S(1)}, bf16[64,512]{1,0:T(8,128)(2,1)S(1)}, u32[]{:S(2)}, u32[]{:S(2)}) collective-permute-start(bf16[64,512]{1,0:T(8,128)(2,1)S(1)} %get-tuple-element.21), channel_id=1, source_target_pairs={{0,8},{4,12},{8,0},{12,4},{1,9},{5,13},{9,1},{13,5},{2,10},{6,14},... | collective-permute-start | bytes 196616 | tf_op jit(solution)/shard_map/ppermute | solution.py:527

commit v3 on v2

--- a/solution.py
+++ b/solution.py
@@ -93,10 +93,11 @@
 
 
 FIRST = ("a1", "a2", "a3", "a4", "g1", "g2", "g3", "g4", "w", "b")
-SECOND = ("a8", "a12", "g8", "g12", "C0", "C1", "C2", "C3", "k4", "b1", "b2")
-BLOCK = ("a", "g", "k", "c", "V0", "V1", "V2", "v0", "v1", "v2")
+SECOND = ("a8", "a12", "g8", "g12", "C0", "C1", "C2", "C3", "k4")
+BLOCK = ("a", "g", "k", "c", "V0", "V1", "V2")
 DOUBLE = ("a", "g", "k", "c")
-READY = ("Z1x", "Z1d", "Z2d")
+TOP = ("a", "g", "k", "wg", "c2")
+READY = ("Zx", "Zd")
 
 
 def first_powers(packed, transition):
@@ -137,7 +138,7 @@
         full, beta = [b[0].astype(F32) + b[1].astype(F32)], [b]
         for i in range(1, 4):
             full.append(mul(b, f["g%d" % i]))
-            beta.append(m.put(("b1", "b2", "C3")[i - 1], full[i]))
+            beta.append(m.put("C3", full[i]) if i == 3 else halves(full[i]))
         a8, g8 = m.put("a8", mul(a4, a4)), m.put("g8", mul(g4, g4))
         c0 = m.put("C0", full[0] + muls((a1, beta[1]), (a2, beta[2]), (a3, beta[3])))
         m.put("C1", full[1] + muls((a1, beta[2]), (a2, beta[3])))
@@ -240,62 +241,80 @@
     )(u, first, second)
 
 
-def block_maps(mats_in, single, after):
-    n = mats_in.shape[2]
-
-    def kernel(mats_ref, single_ref, _, out):
-        f = s = Both(Stack(FIRST, mats_ref), Stack(SECOND, single_ref))
-        mats = Stack(BLOCK, out)
-        k4, a4, g4, a8, g8 = s["k4"], f["a4"], f["g4"], s["a8"], s["g8"]
-        full = [mul(x, k4) for x in (a4, a8, s["a12"])]
-        t = [halves(x) for x in full]
-        mats.put("a", mul(a8, a8))
-        g = mats.put("g", mul(g8, g8))
-        k = k4[0].astype(F32) + k4[1].astype(F32)
-        k = mats.put("k", k + muls((t[0], g4), (t[1], g8), (t[2], s["g12"])))
-        mats.put("V0", full[0] + muls((t[1], g4), (t[2], g8)))
-        mats.put("V1", full[1] + mul(t[2], g4))
-        mats.copy("V2", t[2])
-        mats.put("c", mul(k, g))
-        b, b1, b2, a2, a3 = f["b"], f["b1"], f["b2"], f["a2"], f["a3"]
-        mats.put("v2", mul(a4, b))
-        mats.put("v1", muls((a3, b), (a4, b1)))
-        mats.put("v0", muls((a2, b), (a3, b1), (a4, b2)))
-
-    return pl.pallas_call(
-        kernel,
-        out_shape=stack_shape(BLOCK, n),
+def fill_block(f, mats):
+    k4, a4, g4, a8, g8 = f["k4"], f["a4"], f["g4"], f["a8"], f["g8"]
+    full = [mul(x, k4) for x in (a4, a8, f["a12"])]
+    t = [halves(x) for x in full]
+    mats.put("a", mul(a8, a8))
+    g = mats.put("g", mul(g8, g8))
+    k = k4[0].astype(F32) + k4[1].astype(F32)
+    k = mats.put("k", k + muls((t[0], g4), (t[1], g8), (t[2], f["g12"])))
+    mats.put("V0", full[0] + muls((t[1], g4), (t[2], g8)))
+    mats.put("V1", full[1] + mul(t[2], g4))
+    mats.copy("V2", t[2])
+    mats.put("c", mul(k, g))
+
+
+def fill_double(w, s, mats, top):
+    a, g, k, c = s["a"], s["g"], s["k"], s["c"]
+    mats.put("a", mul(a, a))
+    g = mats.put("g", mul(g, g))
+    k2 = mats.put("k", k[0].astype(F32) + k[1].astype(F32) + mul(a, c))
+    if top:
+        wg = mats.put("wg", mul(w, g))
+        mats.put("c2", c[0].astype(F32) + c[1].astype(F32) + mul(a, wg))
+    else:
+        mats.put("c", mul(k2, g))
+
+
+def all_maps(first, second, after, groups):
+    n = first.shape[2]
+    names = [BLOCK] + [DOUBLE] * (groups - 2) + [TOP]
+
+    def kernel(first_ref, second_ref, _, block):
+        f = Both(Stack(FIRST, first_ref), Stack(SECOND, second_ref))
+        m = Stack(BLOCK, block)
+        fill_block(f, m)
+
+    def both_kernel(first_ref, second_ref, _, block, top):
+        f = Both(Stack(FIRST, first_ref), Stack(SECOND, second_ref))
+        m = Stack(BLOCK, block)
+        fill_block(f, m)
+        fill_double(f["w"], m, Stack(TOP, top), True)
+
+    joined = groups == 2
+    shapes = [stack_shape(names[i], n) for i in range(2 if joined else 1)]
+    maps = pl.pallas_call(
+        both_kernel if joined else kernel,
+        out_shape=shapes,
         in_specs=[VMEM, VMEM, ANY],
-        out_specs=VMEM,
+        out_specs=[VMEM] * len(shapes),
         compiler_params=PARAMS,
         cost_estimate=cost(1.2e9),
         name="block_maps",
-    )(mats_in, single, after)
-
-
-def double_maps(names, given, last):
+    )(first, second, after)
+    maps = list(maps)
+    while len(maps) < groups:
+        maps.append(double_maps(names[len(maps) - 1], maps[-1], first, len(maps) == groups - 1))
+    return maps
+
+
+def double_maps(names, given, first, top):
     n = given.shape[2]
-    kept = DOUBLE[:3] if last else DOUBLE
-
-    def kernel(given_ref, out):
-        s = Stack(names, given_ref)
-        mats = Stack(kept, out)
-        a, g, k = s["a"], s["g"], s["k"]
-        mats.put("a", mul(a, a))
-        g = mats.put("g", mul(g, g))
-        k = mats.put("k", k[0].astype(F32) + k[1].astype(F32) + mul(a, s["c"]))
-        if not last:
-            mats.put("c", mul(k, g))
+    kept = TOP if top else DOUBLE
+
+    def kernel(given_ref, first_ref, out):
+        fill_double(Stack(FIRST, first_ref)["w"], Stack(names, given_ref), Stack(kept, out), top)
 
     return pl.pallas_call(
         kernel,
         out_shape=stack_shape(kept, n),
-        in_specs=[VMEM],
+        in_specs=[VMEM] * 2,
         out_specs=VMEM,
         compiler_params=PARAMS,
         cost_estimate=cost(4e8),
         name="double_maps",
-    )(given)
+    )(given, first)
 
 
 def sides(bit, mine, got):
@@ -330,6 +349,32 @@
     )(bits, mine, got, mats)
 
 
+def last_join(level, names, bits, mine, got, mats, top_mats):
+    members, states = mine.shape[1:]
+
+    def kernel(bits, mine, got, mats_ref, top_ref, end, payload):
+        m, t = Stack(names, mats_ref), Stack(TOP, top_ref)
+        el, er, hl, hr = sides(bits[level], mine, got)
+        pair = halves(el)
+        e = er + mul(pair, m["a"])
+        handed = hl + muls((halves(hr), m["g"]), (pair, t["c2"]), (halves(er), t["wg"]))
+        end[0] = e
+        payload[...] = jnp.where(bits[level + 1] > 0, handed, e).astype(BF16)
+
+    return pl.pallas_call(
+        kernel,
+        out_shape=(
+            jax.ShapeDtypeStruct((1, members, states), F32),
+            jax.ShapeDtypeStruct((members, states), BF16),
+        ),
+        in_specs=[SMEM] + [VMEM] * 4,
+        out_specs=(VMEM, VMEM),
+        compiler_params=PARAMS,
+        cost_estimate=cost(1e8),
+        name="last_join",
+    )(bits, mine, got, mats, top_mats)
+
+
 def either(flag, x, y):
     return tuple(jnp.where(flag, p, q) for p, q in zip(x, y, strict=True))
 
@@ -342,10 +387,10 @@
 
     def kernel(bits, begin, u, e_groups, mats_ref, single_ref, *refs):
         f = Both(Stack(FIRST, mats_ref), Stack(SECOND, single_ref))
-        level_maps = [Stack(BLOCK if i == 0 else DOUBLE, refs[i]) for i in range(top + 1)]
+        level_maps = [Stack(BLOCK if i == 0 else TOP if i == top else DOUBLE, refs[i]) for i in range(top + 1)]
         mine = refs[top + 1 : 2 * top + 2]
         arrived = refs[2 * top + 2 : 3 * top + 2]
-        out_ref, pre, local, local_d = refs[3 * top + 2 :]
+        out_ref, pre, local = refs[3 * top + 2 :]
         mats = Stack(READY, out_ref)
         unit = halves(jnp.eye(states, dtype=F32))
         none = tuple(jnp.zeros_like(x) for x in unit)
@@ -378,7 +423,6 @@
         x0 = begin[...]
         own_e = mine[top][0]
         aw = halves(mul(m["a"], w))
-        wg = halves(mul(w, m["g"]))
         middle = mul(halves(x0), m["a"]) + jnp.where(right, zero, own_e)
         middle_p = halves(middle)
         far = halves(mul(aw, m["g"]) + m["k"][0].astype(F32) + m["k"][1].astype(F32))
@@ -387,22 +431,16 @@
         x_in_p = halves(x_in)
         pre[0] = mul(x_in_p, p) + px
         pre[1] = muls((halves(d_in), q), (x_in_p, r)) + pd
-        mats.copy("Z1x", either(right, p, none))
-        after = mul(either(right, aw, wg), q)
-        after_r = r[0].astype(F32) + r[1].astype(F32)
-        mats.put("Z1d", jnp.where(right, after + after_r, after))
-        mats.copy("Z2d", either(right, none, q))
-        b, b1, b2 = f["b"], f["b1"], f["b2"]
+        mats.copy("Zx", either(right, p, none))
+        near = halves(mul(aw, q) + r[0].astype(F32) + r[1].astype(F32))
+        mats.copy("Zd", either(right, near, q))
         v = u[...].reshape(quads, 4, members, states)
         part = [v[:, j].reshape(-1, states) for j in range(3)]
         pairs = [halves(x) for x in part[:2]]
-        f1 = part[1] + mul(pairs[0], f["a1"])
-        f2 = part[2] + muls((pairs[1], f["a1"]), (pairs[0], f["a2"]))
-        local[0], local[1], local[2], local[3] = part[0], f1, f2, e_groups[...]
-        p1, p2, p3 = halves(f1), halves(f2), halves(e_groups[...])
-        local_d[2] = mul(p3, b)
-        local_d[1] = muls((p2, b), (p3, b1))
-        local_d[0] = muls((p1, b), (p2, b1), (p3, b2))
+        local[0] = part[0]
+        local[1] = part[1] + mul(pairs[0], f["a1"])
+        local[2] = part[2] + muls((pairs[1], f["a1"]), (pairs[0], f["a2"]))
+        local[3] = e_groups[...]
 
     return pl.pallas_call(
         kernel,
@@ -410,30 +448,29 @@
             stack_shape(READY, states),
             jax.ShapeDtypeStruct((2, members, states), F32),
             jax.ShapeDtypeStruct((4, quads * members, states), F32),
-            jax.ShapeDtypeStruct((3, quads * members, states), F32),
         ),
         in_specs=[SMEM] + [VMEM] * (5 + len(maps) + len(ends) + len(got)),
-        out_specs=(VMEM,) * 4,
+        out_specs=(VMEM,) * 3,
         compiler_params=PARAMS,
         cost_estimate=cost(3e9),
         name="ready",
     )(bits, begin, u, e_groups, mats_in, single, *maps, *ends, *got)
 
 
-def finish(bits, got, prepared, pre, local, local_d, x_groups, d_groups, mats, single, block, transition, gain):
+def finish(bits, got, prepared, pre, local, x_groups, d_groups, mats, single, block, transition, gain):
     members, states = pre.shape[1:]
     quads = local.shape[1] // members
     steps = 4 * quads
     groups = bits.shape[0]
 
-    def kernel(bits, got, ready_ref, pre, local, local_d, xg, dg, mats_ref, single_ref, block_ref, tr, ga, *refs):
+    def kernel(bits, got, ready_ref, pre, local, xg, dg, mats_ref, single_ref, block_ref, tr, ga, *refs):
         filtered, smoothed, filtered_held, smoothed_held, sems = refs
         z, m = Stack(READY, ready_ref), Stack(BLOCK, block_ref)
         f = s = Both(Stack(FIRST, mats_ref), Stack(SECOND, single_ref))
-        e, h = got[:, pl.ds(0, states)], got[:, pl.ds(states, states)]
-        exact = lambda x, y: dot(x, y[0]) + dot(x, y[1])
-        x = exact(e, z["Z1x"]) + pre[0]
-        d = exact(e, z["Z1d"]) + exact(h, z["Z2d"]) + pre[1]
+        arrived = got[...]
+        exact = lambda x, y: dot(jnp.concatenate([x, x], 1), jnp.concatenate([y[0], y[1]], 0))
+        x = exact(arrived, z["Zx"]) + pre[0]
+        d = exact(arrived, z["Zd"]) + pre[1]
         xp, dp = halves(x), halves(d)
         ah, gh = [f["a4"], s["a8"], s["a12"]], [f["g4"], s["g8"], s["g12"]]
         xs, ds = [x], []
@@ -443,7 +480,7 @@
             ds.append(dg[part] + muls((dp, gh[quads - q - 1]), (xp, m["V%d" % (q - 1)])))
         x = jnp.concatenate(xs, 0)
         d = jnp.concatenate(ds + [d], 0)
-        xp, dp = halves(x), halves(d)
+        xp = halves(x)
         low = ga[...].astype(BF16)
         final = bits[0] > 0
         for i in range(1, groups):
@@ -468,18 +505,18 @@
             states_of.append(value)
             write(filtered_held, j, value)
         copies = send(filtered_held, filtered, sems.at[0])
+        adjusted = []
         for j in range(4):
-            value = states_of[j]
-            if j < 3:
-                handed = local_d[j] + muls((dp, f["g%d" % (3 - j)]), (xp, m["v%d" % j]))
-            else:
-                handed = d
-            predicted = dot_nt(value.astype(BF16), tr[...]).astype(BF16)
-            result = value - dot_nt(predicted, low) + handed
-            if j == 3:
-                tail = (quads - 1) * members
-                result = jnp.concatenate([result[:tail], jnp.where(final, value[tail:], result[tail:])], 0)
-            write(smoothed_held, j, result)
+            predicted = dot_nt(states_of[j].astype(BF16), tr[...]).astype(BF16)
+            adjusted.append(states_of[j] - dot_nt(predicted, low))
+        result = adjusted[3] + d
+        tail = (quads - 1) * members
+        result = jnp.concatenate([result[:tail], jnp.where(final, states_of[3][tail:], result[tail:])], 0)
+        write(smoothed_held, 3, result)
+        later = [halves(adjusted[1]), halves(adjusted[2]), halves(result)]
+        for j in range(3):
+            handed = muls(*((later[i - 1], f["g%d" % (i - j)]) for i in range(j + 1, 4)))
+            write(smoothed_held, j, adjusted[j] + handed)
         copies += send(smoothed_held, smoothed, sems.at[1])
         for copy in copies:
             copy.wait()
@@ -487,7 +524,7 @@
     return pl.pallas_call(
         kernel,
         out_shape=(jax.ShapeDtypeStruct((members * steps, states), F32),) * 2,
-        in_specs=[SMEM] + [VMEM] * 12,
+        in_specs=[SMEM] + [VMEM] * 11,
         out_specs=(ANY,) * 2,
         scratch_shapes=[
             pltpu.VMEM((states // LANES, members * steps, LANES), F32),
@@ -497,7 +534,7 @@
         compiler_params=PARAMS,
         cost_estimate=cost(3e9),
         name="finish",
-    )(bits, got, prepared, pre, local, local_d, x_groups, d_groups, mats, single, block, transition, gain)
+    )(bits, got, prepared, pre, local, x_groups, d_groups, mats, single, block, transition, gain)
 
 
 def body(observations, obs_gain, closed_loop, transition, smoother_gain, initial_mean):
@@ -506,7 +543,7 @@
     assert steps == 16
     blocks = lax.axis_size("tm")
     groups = blocks.bit_length() - 1
-    assert blocks == 1 << groups
+    assert blocks == 1 << groups and groups >= 2
     place = lax.axis_index("sens").astype(jnp.int32).reshape(1)
     position = lax.axis_index("tm").astype(jnp.int32)
     bits = jnp.stack([(position >> i) & 1 for i in range(groups)])
@@ -518,22 +555,24 @@
     mats = first_powers(packed, transition)
     single, u = second_powers(mats, own, other)
     e_groups, x_groups, d_groups, ends, payload = up(u, mats, single, members)
-    block = block_maps(mats, single, ends)
-    maps = [block]
-    for i in range(1, groups):
-        maps.append(double_maps(BLOCK if i == 1 else DOUBLE, maps[-1], i == groups - 1))
+    maps = all_maps(mats, single, ends, groups)
+    block = maps[0]
     mine, got = [ends], []
     for i in range(groups):
         arrived = lax.ppermute(payload, "tm", [(j, j ^ (1 << i)) for j in range(blocks)])
         got.append(arrived)
-        if i < groups - 1:
-            ends, payload = join(i, BLOCK if i == 0 else DOUBLE, bits, ends, arrived, maps[i])
+        names = BLOCK if i == 0 else DOUBLE
+        if i < groups - 2:
+            ends, payload = join(i, names, bits, ends, arrived, maps[i])
             mine.append(ends)
-    prepared, pre, local, local_d = ready(
+        elif i == groups - 2:
+            ends, payload = last_join(i, names, bits, ends, arrived, maps[i], maps[i + 1])
+            mine.append(ends)
+    prepared, pre, local = ready(
         bits, initial_mean, u, e_groups, mats, single, maps, mine, got[:-1]
     )
     filtered, smoothed = finish(
-        bits, got[-1], prepared, pre, local, local_d, x_groups, d_groups, mats, single, block, transition, smoother_gain
+        bits, got[-1], prepared, pre, local, x_groups, d_groups, mats, single, block, transition, smoother_gain
     )
     shape = (members, steps, states)
     return filtered.reshape(shape), smoothed.reshape(shape)

time: 27.8 us -> 27 us (0.971)
  Pallas kernels: 17.5 us -> 16.3 us
    pallas_call x1, Pallas kernels: 2.83 us -> 2.13 us  [ready(): pl.pallas_call(kernel, out_shape=(stack_shape(READY, states), jax.ShapeDt...]
    pallas_call x1, Pallas kernels: 4.94 us -> 4.65 us  [finish(): pl.pallas_call(kernel, out_shape=(jax.ShapeDtypeStruct((members * steps,...]
    pallas_call x3 -> x2, Pallas kernels: 3.47 us -> 3.37 us  [the longest x1 2.44 us: all_maps(): pl.pallas_call(both_kernel if joined else kernel, out_shape=shapes, in_sp...]
  transfers between devices with their start and end apart: 3 -> 3, of which waited for: 0 -> 0; matrix products, arithmetic and copies ran while one was open for 0% -> 0% of each run, Pallas kernels for 26% -> 24%
where the time goes in v3:
time: 27 us; the launch traced here: 26.8 us
  Pallas kernels  16.3 us (60%)
  starting transfers between devices  6.49 us (24%)
  local copies, waits for them, and re-layouts  3.03 us (11%)
  between operations  0.77 us (3%)
    ppermute x2, starting transfers between devices, body(): lax.ppermute(payload, 'tm', [(j, j ^ 1 << i) for j in range(blocks)])  5.97 us
    pallas_call x1, Pallas kernels, finish(): pl.pallas_call(kernel, out_shape=(jax.ShapeDtypeStruct((members * steps,...  4.65 us
    unnamed x16, local copies, waits for them, and re-layouts  3.03 us
    pallas_call x1, Pallas kernels, all_maps(): pl.pallas_call(both_kernel if joined else kernel, out_shape=shapes, in_sp...  2.44 us
    pallas_call x1, Pallas kernels, ready(): pl.pallas_call(kernel, out_shape=(stack_shape(READY, states), jax.ShapeDt...  2.13 us
    pallas_call x1, Pallas kernels, up(): pl.pallas_call(kernel, out_shape=(jax.ShapeDtypeStruct((quads * members,...  1.89 us
    pallas_call x1, Pallas kernels, second_powers(): pl.pallas_call(kernel, out_shape=(stack_shape(SECOND, n), jax.ShapeDtypeS...  1.77 us
    pallas_call x2, Pallas kernels, half_inputs(): pl.pallas_call(kernel, out_shape=jax.ShapeDtypeStruct((members * steps, s...  1.44 us
  transfers between devices with their start and end apart: 3, of which 0 were waited for; matrix products, arithmetic and copies ran while one was open for 0% of the time, Pallas kernels for 24%

profile of v3, /device:TPU:0, one launch (start us, length us, event | category | flops | bytes accessed | tf_op | source)
XLA Modules:
  0.0 26.8 jit_solution(6641077628996858085)
XLA Ops:
  0.6 0.0 copy-start
  0.6 1.6 %copy-done = bf16[128,16,512]{2,1,0:T(8,128)(2,1)S(1)} copy-done((bf16[128,16,512]{2,1,0:T(8,128)(2,1)S(1)}, bf16[128,16,512]{2,1,0:T(8,128)(2,1)}, u32[]{:S(2)}) %copy-start) | copy-done | bytes 2097176
  2.2 0.0 copy-start.2
  2.2 0.9 %copy-done.2 = bf16[256,512]{1,0:T(8,128)(2,1)S(1)} copy-done((bf16[256,512]{1,0:T(8,128)(2,1)S(1)}, bf16[256,512]{1,0:T(8,128)(2,1)}, u32[]{:S(2)}) %copy-start.2) | copy-done | bytes 262168
  3.2 0.0 copy-start.1
  3.2 0.0 copy-start.3
  3.2 0.7 %inputs_other.1 = bf16[1024,256]{1,0:T(8,128)(2,1)S(1)} custom-call(s32[1]{0:T(128)} %bitcast.4.place, bf16[128,16,512]{2,1,0:T(8,128)(2,1)S(1)} %copy-done, bf16[256,512]{1,0:T(8,128)(2,1)S(1)} %copy-done.2), custom_call_target="tpu_custom_call" | custom-call | flops 268435456 | tf_op jit(solution)/shard_map/inputs_other/pallas_call | solution.py:177
  3.9 0.0 copy-start.4
  3.9 0.0 copy-start.7
  4.0 0.5 %collective-permute-start = (bf16[1024,256]{1,0:T(8,128)(2,1)S(1)}, bf16[1024,256]{1,0:T(8,128)(2,1)}, u32[]{:S(2)}, u32[]{:S(2)}) collective-permute-start(bf16[1024,256]{1,0:T(8,128)(2,1)S(1)} %inputs_other.1), channel_id=1, source_target_pairs={{0,1},{1,0},{2,3},{3,2},{4,5},{5,4},{6,7},{7,6},{8,9},{9,8},{10,11... | collective-permute-start | bytes 1572872 | tf_op jit(solution)/shard_map/ppermute | solution.py:553
  4.5 0.3 %copy-done.1 = bf16[128,16,512]{2,1,0:T(8,128)(2,1)S(1)} copy-done((bf16[128,16,512]{2,1,0:T(8,128)(2,1)S(1)}, bf16[128,16,512]{2,1,0:T(8,128)(2,1)}, u32[]{:S(2)}) %copy-start.1) | copy-done | bytes 2097176
  4.8 0.0 copy-done.3
  4.8 0.0 copy-start.5
  4.8 0.7 %inputs_own.1.own = f32[1024,256]{1,0:T(8,128)S(1)} custom-call(s32[1]{0:T(128)} %bitcast.4.place, bf16[128,16,512]{2,1,0:T(8,128)(2,1)S(1)} %copy-done.1, bf16[256,512]{1,0:T(8,128)(2,1)S(1)} %copy-done.3), custom_call_target="tpu_custom_call" | custom-call | flops 268435456 | tf_op jit(solution)/shard_map/inputs_own/pallas_call | solution.py:177
  5.5 0.0 copy-done.4
  5.5 0.0 copy-done.7
  5.5 0.2 copy-done.5
  5.7 1.1 %first_powers.1.first_ref.mats_ref = bf16[10,2,256,256]{3,2,1,0:T(8,128)(2,1)S(1)} custom-call(f32[2,256,256]{2,1,0:T(8,128)S(1)} %pad_maximum_fusion.packed, bf16[256,256]{1,0:T(8,128)(2,1)S(1)} %copy-done.5), custom_call_target="tpu_custom_call" | custom-call | flops 1000000000 | tf_op jit(solution)/shard_map/first_powers/pallas_call | solution.py:119
  6.8 0.1 pad_add_fusion.bits
  6.9 0.0 collective-permute-done.other
  6.9 1.8 %second_powers.1 = (bf16[9,2,256,256]{3,2,1,0:T(8,128)(2,1)S(1)}, f32[1024,256]{1,0:T(8,128)S(1)}) custom-call(bf16[10,2,256,256]{3,2,1,0:T(8,128)(2,1)S(1)} %first_powers.1.first_ref.mats_ref, f32[1024,256]{1,0:T(8,128)S(1)} %inputs_own.1.own, bf16[1024,256]{1,0:T(8,128)(2,1)} %collective-permute-done.other), custom_call_target="tpu_custom_call" | custom-call | flops 1500000000 | tf_op jit(solution)/shard_map/second_powers/pallas_call | solution.py:152
  8.7 1.9 %up.1 = (f32[256,256]{1,0:T(8,128)S(1)}, f32[192,256]{1,0:T(8,128)S(1)}, f32[192,256]{1,0:T(8,128)S(1)}, f32[2,64,256]{2,1,0:T(8,128)S(1)}, bf16[64,512]{1,0:T(8,128)(2,1)S(1)}) custom-call(f32[1024,256]{1,0:T(8,128)S(1)} %get-tuple-element.18.u, bf16[10,2,256,256]{3,2,1,0:T(8,128)(2,1)S(1)} %first_powers.1.first_ref.mats_ref, ...), custom_call_target="tpu_custom_call" | custom-call | flops 2000000000 | tf_op jit(solution)/shard_map/up/pallas_call | solution.py:227
  10.6 3.1 %collective-permute-start.1 = (bf16[64,512]{1,0:T(8,128)(2,1)S(1)}, bf16[64,512]{1,0:T(8,128)(2,1)S(1)}, u32[]{:S(2)}, u32[]{:S(2)}) collective-permute-start(bf16[64,512]{1,0:T(8,128)(2,1)S(1)} %get-tuple-element.21), channel_id=1, source_target_pairs={{0,4},{4,0},{8,12},{12,8},{1,5},{5,1},{9,13},{13,9},{2,6},{6,2},{1... | collective-permute-start | bytes 196616 | tf_op jit(solution)/shard_map/ppermute | solution.py:562
  13.7 2.4 %block_maps.1 = (bf16[7,2,256,256]{3,2,1,0:T(8,128)(2,1)S(1)}, bf16[5,2,256,256]{3,2,1,0:T(8,128)(2,1)S(1)}) custom-call(bf16[10,2,256,256]{3,2,1,0:T(8,128)(2,1)S(1)} %first_powers.1.first_ref.mats_ref, bf16[9,2,256,256]{3,2,1,0:T(8,128)(2,1)S(1)} %get-tuple-element.19.second_ref.single_ref, f32[2,64,256]{2,1,0:T(8,128)S(1)} %get-tuple-element.20._.mine.refs_2_), custom_call_target="tpu_custom_call" | custom-call | flops 1200000000 | tf_op jit(solution)/shard_map/block_maps/pallas_call | solution.py:287
  16.1 0.0 copy-start.6
  16.1 0.0 collective-permute-done.1.got.refs_4_
  16.1 0.9 %last_join.1 = (f32[1,64,256]{2,1,0:T(8,128)S(1)}, bf16[64,256]{1,0:T(8,128)(2,1)S(1)}) custom-call(s32[2]{0:T(128)S(1)} %pad_add_fusion.bits, f32[2,64,256]{2,1,0:T(8,128)S(1)} %get-tuple-element.20._.mine.refs_2_, bf16[64,512]{1,0:T(8,128)(2,1)S(1)} %collective-permute-done.1.got.refs_4_, ...), custom_call_target="tpu_custom_call" | custom-call | flops 100000000 | tf_op jit(solution)/shard_map/last_join/pallas_call | solution.py:364
  17.1 2.9 %collective-permute-start.2 = (bf16[64,256]{1,0:T(8,128)(2,1)S(1)}, bf16[64,256]{1,0:T(8,128)(2,1)S(1)}, u32[]{:S(2)}, u32[]{:S(2)}) collective-permute-start(bf16[64,256]{1,0:T(8,128)(2,1)S(1)} %get-tuple-element.24), channel_id=1, source_target_pairs={{0,8},{4,12},{8,0},{12,4},{1,9},{5,13},{9,1},{13,5},{2,10},{6,14},... | collective-permute-start | bytes 98312 | tf_op jit(solution)/shard_map/ppermute | solution.py:562
  20.0 0.0 copy-done.6
  20.0 2.1 %ready.1 = (bf16[2,2,256,256]{3,2,1,0:T(8,128)(2,1)S(1)}, f32[2,64,256]{2,1,0:T(8,128)S(1)}, f32[4,256,256]{2,1,0:T(8,128)S(1)}) custom-call(s32[2]{0:T(128)S(1)} %pad_add_fusion.bits, f32[64,256]{1,0:T(8,128)S(1)} %copy-done.6, f32[1024,256]{1,0:T(8,128)S(1)} %get-tuple-element.18.u, f32[256,256]{1,0:T(8,128)S(1)} %get-tuple-element.25.e_groups, ...), custom_call_target="tpu_custom_call" | custom-call | flops 3000000000 | tf_op jit(solution)/shard_map/ready/pallas_call | solution.py:445
  22.1 0.0 collective-permute-done.2.got
  22.1 4.7 %finish.1 = (f32[1024,256]{1,0:T(8,128)}, f32[1024,256]{1,0:T(8,128)}) custom-call(s32[2]{0:T(128)S(1)} %pad_add_fusion.bits, bf16[64,256]{1,0:T(8,128)(2,1)S(1)} %collective-permute-done.2.got, bf16[2,2,256,256]{3,2,1,0:T(8,128)(2,1)S(1)} %get-tuple-element.27.ready_ref, f32[2,64,256]{2,1,0:T(8,128)S(1)} %get-tuple-element.28.pre, ...), custom_call_target="tpu_custom_call" | custom-call | flops 3000000000 | tf_op jit(solution)/shard_map/finish/pallas_call | solution.py:524
  (1 shorter events, 0.0 us)
Async XLA Ops:
  0.6 1.6 %copy-start = (bf16[128,16,512]{2,1,0:T(8,128)(2,1)S(1)}, bf16[128,16,512]{2,1,0:T(8,128)(2,1)}, u32[]{:S(2)}) copy-start(bf16[128,16,512]{2,1,0:T(8,128)(2,1)} %obs.3) | copy-start | bytes 6291460
  2.2 0.9 %copy-start.2 = (bf16[256,512]{1,0:T(8,128)(2,1)S(1)}, bf16[256,512]{1,0:T(8,128)(2,1)}, u32[]{:S(2)}) copy-start(bf16[256,512]{1,0:T(8,128)(2,1)} %gain.3) | copy-start | bytes 786436
  3.2 1.6 %copy-start.1 = (bf16[128,16,512]{2,1,0:T(8,128)(2,1)S(1)}, bf16[128,16,512]{2,1,0:T(8,128)(2,1)}, u32[]{:S(2)}) copy-start(bf16[128,16,512]{2,1,0:T(8,128)(2,1)} %obs.3) | copy-start | bytes 6291460
  3.2 1.6 %copy-start.3 = (bf16[256,512]{1,0:T(8,128)(2,1)S(1)}, bf16[256,512]{1,0:T(8,128)(2,1)}, u32[]{:S(2)}) copy-start(bf16[256,512]{1,0:T(8,128)(2,1)} %gain.3) | copy-start | bytes 786436
  3.9 1.6 %copy-start.4 = (f32[256,256]{1,0:T(8,128)S(1)}, f32[256,256]{1,0:T(8,128)}, u32[]{:S(2)}) copy-start(f32[256,256]{1,0:T(8,128)} %ga.1) | copy-start | bytes 786436
  3.9 1.6 %copy-start.7 = (f32[256,256]{1,0:T(8,128)S(1)}, f32[256,256]{1,0:T(8,128)}, u32[]{:S(2)}) copy-start(f32[256,256]{1,0:T(8,128)} %param.8) | copy-start | bytes 786436
  4.0 2.9 %collective-permute-start = (bf16[1024,256]{1,0:T(8,128)(2,1)S(1)}, bf16[1024,256]{1,0:T(8,128)(2,1)}, u32[]{:S(2)}, u32[]{:S(2)}) collective-permute-start(bf16[1024,256]{1,0:T(8,128)(2,1)S(1)} %inputs_other.1), channel_id=1, source_target_pairs={{0,1},{1,0},{2,3},{3,2},{4,5},{5,4},{6,7},{7,6},{8,9},{9,8},{10,11... | collective-permute-start | bytes 1572872 | tf_op jit(solution)/shard_map/ppermute | solution.py:553
  4.8 0.9 %copy-start.5 = (bf16[256,256]{1,0:T(8,128)(2,1)S(1)}, bf16[256,256]{1,0:T(8,128)(2,1)}, u32[]{:S(2)}) copy-start(bf16[256,256]{1,0:T(8,128)(2,1)} %tr.3) | copy-start | bytes 393220
  10.6 5.6 %collective-permute-start.1 = (bf16[64,512]{1,0:T(8,128)(2,1)S(1)}, bf16[64,512]{1,0:T(8,128)(2,1)S(1)}, u32[]{:S(2)}, u32[]{:S(2)}) collective-permute-start(bf16[64,512]{1,0:T(8,128)(2,1)S(1)} %get-tuple-element.21), channel_id=1, source_target_pairs={{0,4},{4,0},{8,12},{12,8},{1,5},{5,1},{9,13},{13,9},{2,6},{6,2},{1... | collective-permute-start | bytes 196616 | tf_op jit(solution)/shard_map/ppermute | solution.py:562
  16.1 3.8 %copy-start.6 = (f32[64,256]{1,0:T(8,128)S(1)}, f32[64,256]{1,0:T(8,128)}, u32[]{:S(2)}) copy-start(f32[64,256]{1,0:T(8,128)} %begin.1) | copy-start | bytes 196612
  17.1 5.0 %collective-permute-start.2 = (bf16[64,256]{1,0:T(8,128)(2,1)S(1)}, bf16[64,256]{1,0:T(8,128)(2,1)S(1)}, u32[]{:S(2)}, u32[]{:S(2)}) collective-permute-start(bf16[64,256]{1,0:T(8,128)(2,1)S(1)} %get-tuple-element.24), channel_id=1, source_target_pairs={{0,8},{4,12},{8,0},{12,4},{1,9},{5,13},{9,1},{13,5},{2,10},{6,14},... | collective-permute-start | bytes 98312 | tf_op jit(solution)/shard_map/ppermute | solution.py:562

commit v4 on v3

--- a/solution.py
+++ b/solution.py
@@ -12,6 +12,7 @@
 SMEM = pl.BlockSpec(memory_space=pltpu.SMEM)
 ANY = pl.BlockSpec(memory_space=pl.ANY)
 PARAMS = pltpu.CompilerParams(vmem_limit_bytes=24 * 2**20)
+WIDE = pltpu.CompilerParams(vmem_limit_bytes=54 * 2**20)
 
 
 def halves(x):
@@ -100,13 +101,14 @@
 READY = ("Zx", "Zd")
 
 
-def first_powers(packed, transition):
-    n = packed.shape[2]
-
-    def kernel(packed, tr, out):
+def first_powers(loop, gain, transition):
+    n = loop.shape[0]
+
+    def kernel(loop, gain, tr, out, token):
+        token[...] = jnp.zeros(token.shape, F32)
         m = Stack(FIRST, out)
-        a1 = m.put("a1", packed[0].T)
-        g_full = packed[1].T
+        a1 = m.put("a1", loop[...].T)
+        g_full = gain[...].T
         g1 = m.put("g1", g_full)
         w = m.put("w", dot(tr[...].T, g1[0]))
         a2, g2 = m.put("a2", mul(a1, a1)), m.put("g2", mul(g1, g1))
@@ -118,13 +120,13 @@
 
     return pl.pallas_call(
         kernel,
-        out_shape=stack_shape(FIRST, n),
-        in_specs=[VMEM, VMEM],
-        out_specs=VMEM,
+        out_shape=(stack_shape(FIRST, n), jax.ShapeDtypeStruct((8, LANES), F32)),
+        in_specs=[VMEM] * 3,
+        out_specs=(VMEM, VMEM),
         compiler_params=PARAMS,
         cost_estimate=cost(1e9),
         name="first_powers",
-    )(packed, transition)
+    )(loop, gain, transition)
 
 
 def second_powers(first, own, other):
@@ -161,29 +163,68 @@
     )(first, own, other)
 
 
-def half_inputs(place, obs, gain, members, sign, dtype):
+def other_inputs(place, obs, gain, members):
+    steps, sensors = obs.shape[1:]
+    states = gain.shape[0]
+    rows = members * steps
+
+    def kernel(place, obs, gain, send, og, read, held, stage, sems):
+        copies = [
+            pltpu.make_async_copy(gain, og, sems.at[0]),
+            pltpu.make_async_copy(obs.at[pl.ds((1 - place[0]) * members, members)], read, sems.at[1]),
+        ]
+        for copy in copies:
+            copy.start()
+        for copy in copies:
+            copy.wait()
+        cut = 16
+        for i in range(members // cut):
+            part = read[pl.ds(i * cut, cut)].reshape(cut * steps, sensors)
+            split_cols(held, i * cut * steps, dot_nt(part, og[...]))
+        by_step(held, stage, members, steps)
+        last = pltpu.make_async_copy(stage, send, sems.at[2])
+        last.start()
+        last.wait()
+
+    return pl.pallas_call(
+        kernel,
+        out_shape=jax.ShapeDtypeStruct((rows, states), BF16),
+        in_specs=[SMEM, ANY, ANY],
+        out_specs=ANY,
+        scratch_shapes=[
+            pltpu.VMEM(gain.shape, BF16),
+            pltpu.VMEM((members, steps, sensors), BF16),
+            pltpu.VMEM((states // LANES, rows, LANES), F32),
+            pltpu.VMEM((rows, states), BF16),
+            pltpu.SemaphoreType.DMA((3,)),
+        ],
+        compiler_params=WIDE,
+        cost_estimate=cost(5e8),
+        name="other_inputs",
+    )(place, obs, gain)
+
+
+def own_inputs(place, obs, gain, after, members):
     steps, sensors = obs.shape[1:]
     states = gain.shape[0]
     cut = 16
-    rows = cut * steps
-
-    def kernel(place, obs, gain, out, held):
-        half = place[0] if sign > 0 else 1 - place[0]
+
+    def kernel(place, obs, gain, _, out, held):
         for i in range(members // cut):
-            part = obs[pl.ds(half * members + i * cut, cut)].reshape(rows, sensors)
-            split_cols(held, i * rows, dot_nt(part, gain[...]))
+            part = obs[pl.ds(place[0] * members + i * cut, cut)].reshape(cut * steps, sensors)
+            split_cols(held, i * cut * steps, dot_nt(part, gain[...]))
         by_step(held, out, members, steps)
 
     return pl.pallas_call(
         kernel,
-        out_shape=jax.ShapeDtypeStruct((members * steps, states), dtype),
-        in_specs=[SMEM, VMEM, VMEM],
+        out_shape=jax.ShapeDtypeStruct((members * steps, states), F32),
+        in_specs=[SMEM, VMEM, VMEM, ANY],
         out_specs=VMEM,
         scratch_shapes=[pltpu.VMEM((states // LANES, members * steps, LANES), F32)],
         compiler_params=PARAMS,
-        cost_estimate=cost(2 * rows * sensors * states * 4),
-        name="inputs_own" if sign > 0 else "inputs_other",
-    )(place, obs, gain)
+        cost_estimate=cost(5e8),
+        name="own_inputs",
+    )(place, obs, gain, after)
 
 
 def put_payload(payload, e, h):
@@ -548,11 +589,10 @@
     position = lax.axis_index("tm").astype(jnp.int32)
     bits = jnp.stack([(position >> i) & 1 for i in range(groups)])
 
-    packed = jnp.stack([closed_loop, smoother_gain])
-    to_send = half_inputs(place, observations, obs_gain, members, -1, BF16)
+    to_send = other_inputs(place, observations, obs_gain, members)
     other = lax.ppermute(to_send, "sens", [(0, 1), (1, 0)])
-    own = half_inputs(place, observations, obs_gain, members, 1, F32)
-    mats = first_powers(packed, transition)
+    mats, token = first_powers(closed_loop, smoother_gain, transition)
+    own = own_inputs(place, observations, obs_gain, token, members)
     single, u = second_powers(mats, own, other)
     e_groups, x_groups, d_groups, ends, payload = up(u, mats, single, members)
     maps = all_maps(mats, single, ends, groups)

time: 27 us -> 26.1 us (0.967)
  local copies, waits for them, and re-layouts: 3.03 us -> 0.03 us
  Pallas kernels: 16.3 us -> 18.6 us
    unnamed x16 -> x12, local copies, waits for them, and re-layouts: 3.03 us -> 0.03 us
    pallas_call x3, Pallas kernels: 2.54 us -> 4.72 us  [the longest x1 2.92 us: other_inputs(): pl.pallas_call(kernel, out_shape=jax.ShapeDtypeStruct((rows, states), BF1...]
  transfers between devices with their start and end apart: 3 -> 3, of which waited for: 0 -> 0; matrix products, arithmetic and copies ran while one was open for 0% -> 0% of each run, Pallas kernels for 24% -> 25%
where the time goes in v4:
time: 26.1 us; the launch traced here: 25.9 us
  Pallas kernels  18.6 us (71%)
  starting transfers between devices  6.4 us (25%)
  between operations  0.78 us (3%)
    ppermute x2, starting transfers between devices, body(): lax.ppermute(payload, 'tm', [(j, j ^ 1 << i) for j in range(blocks)])  5.88 us
    pallas_call x1, Pallas kernels, finish(): pl.pallas_call(kernel, out_shape=(jax.ShapeDtypeStruct((members * steps,...  4.66 us
    pallas_call x1, Pallas kernels, other_inputs(): pl.pallas_call(kernel, out_shape=jax.ShapeDtypeStruct((rows, states), BF1...  2.92 us
    pallas_call x1, Pallas kernels, all_maps(): pl.pallas_call(both_kernel if joined else kernel, out_shape=shapes, in_sp...  2.44 us
    pallas_call x1, Pallas kernels, ready(): pl.pallas_call(kernel, out_shape=(stack_shape(READY, states), jax.ShapeDt...  2.14 us
    pallas_call x1, Pallas kernels, up(): pl.pallas_call(kernel, out_shape=(jax.ShapeDtypeStruct((quads * members,...  1.89 us
    pallas_call x1, Pallas kernels, second_powers(): pl.pallas_call(kernel, out_shape=(stack_shape(SECOND, n), jax.ShapeDtypeS...  1.85 us
    pallas_call x1, Pallas kernels, first_powers(): pl.pallas_call(kernel, out_shape=(stack_shape(FIRST, n), jax.ShapeDtypeSt...  1.1 us
  transfers between devices with their start and end apart: 3, of which 0 were waited for; matrix products, arithmetic and copies ran while one was open for 0% of the time, Pallas kernels for 25%

profile of v4, /device:TPU:0, one launch (start us, length us, event | category | flops | bytes accessed | tf_op | source)
XLA Modules:
  0.0 25.9 jit_solution(4204308620048043922)
XLA Ops:
  0.6 0.0 copy-start.3
  0.6 0.0 copy-start.4
  0.7 0.0 copy-start.2
  0.7 2.9 %other_inputs.1 = bf16[1024,256]{1,0:T(8,128)(2,1)} custom-call(s32[1]{0:T(128)} %bitcast.2.place, bf16[128,16,512]{2,1,0:T(8,128)(2,1)} %obs.3, bf16[256,512]{1,0:T(8,128)(2,1)} %gain.5), custom_call_target="tpu_custom_call" | custom-call | flops 500000000 | tf_op jit(solution)/shard_map/other_inputs/pallas_call | solution.py:189
  3.6 0.0 copy-start
  3.6 0.0 copy-start.1
  3.6 0.5 %collective-permute-start = (bf16[1024,256]{1,0:T(8,128)(2,1)}, bf16[1024,256]{1,0:T(8,128)(2,1)S(1)}, u32[]{:S(2)}, u32[]{:S(2)}) collective-permute-start(bf16[1024,256]{1,0:T(8,128)(2,1)} %other_inputs.1), channel_id=1, source_target_pairs={{0,1},{1,0},{2,3},{3,2},{4,5},{5,4},{6,7},{7,6},{8,9},{9,8},{10,11... | collective-permute-start | bytes 1572872 | tf_op jit(solution)/shard_map/ppermute | solution.py:593
  4.1 0.0 copy-done.3
  4.1 0.0 copy-done.4
  4.1 0.0 copy-done.2
  4.1 1.1 %first_powers.1 = (bf16[10,2,256,256]{3,2,1,0:T(8,128)(2,1)S(1)}, f32[8,128]{1,0:T(8,128)S(1)}) custom-call(f32[256,256]{1,0:T(8,128)S(1)} %copy-done.2, f32[256,256]{1,0:T(8,128)S(1)} %copy-done.3, bf16[256,256]{1,0:T(8,128)(2,1)S(1)} %copy-done.4), custom_call_target="tpu_custom_call" | custom-call | flops 1000000000 | tf_op jit(solution)/shard_map/first_powers/pallas_call | solution.py:121
  5.2 0.0 copy-done
  5.3 0.0 copy-done.1
  5.3 0.7 %own_inputs.1.own = f32[1024,256]{1,0:T(8,128)S(1)} custom-call(s32[1]{0:T(128)} %bitcast.2.place, bf16[128,16,512]{2,1,0:T(8,128)(2,1)S(1)} %copy-done, bf16[256,512]{1,0:T(8,128)(2,1)S(1)} %copy-done.1, f32[8,128]{1,0:T(8,128)S(1)} %get-tuple-element.21._), custom_call_target="tpu_custom_call" | custom-call | flops 500000000 | tf_op jit(solution)/shard_map/own_inputs/pallas_call | solution.py:218
  6.0 0.1 pad_add_fusion.bits
  6.1 0.0 collective-permute-done.other
  6.1 1.9 %second_powers.1 = (bf16[9,2,256,256]{3,2,1,0:T(8,128)(2,1)S(1)}, f32[1024,256]{1,0:T(8,128)S(1)}) custom-call(bf16[10,2,256,256]{3,2,1,0:T(8,128)(2,1)S(1)} %get-tuple-element.20.first_ref.mats_ref, f32[1024,256]{1,0:T(8,128)S(1)} %own_inputs.1.own, bf16[1024,256]{1,0:T(8,128)(2,1)S(1)} %collective-permute-done.other), custom_call_target="tpu_custom_call" | custom-call | flops 1500000000 | tf_op jit(solution)/shard_map/second_powers/pallas_call | solution.py:154
  7.9 1.9 %up.1 = (f32[256,256]{1,0:T(8,128)S(1)}, f32[192,256]{1,0:T(8,128)S(1)}, f32[192,256]{1,0:T(8,128)S(1)}, f32[2,64,256]{2,1,0:T(8,128)S(1)}, bf16[64,512]{1,0:T(8,128)(2,1)S(1)}) custom-call(f32[1024,256]{1,0:T(8,128)S(1)} %get-tuple-element.22.u, bf16[10,2,256,256]{3,2,1,0:T(8,128)(2,1)S(1)} %get-tuple-element.20.first_ref.mats_ref, ...), custom_call_target="tpu_custom_call" | custom-call | flops 2000000000 | tf_op jit(solution)/shard_map/up/pallas_call | solution.py:268
  9.8 3.0 %collective-permute-start.1 = (bf16[64,512]{1,0:T(8,128)(2,1)S(1)}, bf16[64,512]{1,0:T(8,128)(2,1)S(1)}, u32[]{:S(2)}, u32[]{:S(2)}) collective-permute-start(bf16[64,512]{1,0:T(8,128)(2,1)S(1)} %get-tuple-element.25), channel_id=1, source_target_pairs={{0,4},{4,0},{8,12},{12,8},{1,5},{5,1},{9,13},{13,9},{2,6},{6,2},{1... | collective-permute-start | bytes 196616 | tf_op jit(solution)/shard_map/ppermute | solution.py:602
  12.8 2.4 %block_maps.1 = (bf16[7,2,256,256]{3,2,1,0:T(8,128)(2,1)S(1)}, bf16[5,2,256,256]{3,2,1,0:T(8,128)(2,1)S(1)}) custom-call(bf16[10,2,256,256]{3,2,1,0:T(8,128)(2,1)S(1)} %get-tuple-element.20.first_ref.mats_ref, bf16[9,2,256,256]{3,2,1,0:T(8,128)(2,1)S(1)} %get-tuple-element.23.second_ref.single_ref, f32[2,64,256]{2,1,0:T(8,128)S(1)} %get-tuple-element.24._.mine.refs_2_), custom_call_target="tpu_custom_call" | custom-call | flops 1200000000 | tf_op jit(solution)/shard_map/block_maps/pallas_call | solution.py:328
  15.3 0.0 copy-start.5
  15.3 0.0 collective-permute-done.1.got.refs_4_
  15.3 0.9 %last_join.1 = (f32[1,64,256]{2,1,0:T(8,128)S(1)}, bf16[64,256]{1,0:T(8,128)(2,1)S(1)}) custom-call(s32[2]{0:T(128)S(1)} %pad_add_fusion.bits, f32[2,64,256]{2,1,0:T(8,128)S(1)} %get-tuple-element.24._.mine.refs_2_, bf16[64,512]{1,0:T(8,128)(2,1)S(1)} %collective-permute-done.1.got.refs_4_, ...), custom_call_target="tpu_custom_call" | custom-call | flops 100000000 | tf_op jit(solution)/shard_map/last_join/pallas_call | solution.py:405
  16.2 2.9 %collective-permute-start.2 = (bf16[64,256]{1,0:T(8,128)(2,1)S(1)}, bf16[64,256]{1,0:T(8,128)(2,1)S(1)}, u32[]{:S(2)}, u32[]{:S(2)}) collective-permute-start(bf16[64,256]{1,0:T(8,128)(2,1)S(1)} %get-tuple-element.28), channel_id=1, source_target_pairs={{0,8},{4,12},{8,0},{12,4},{1,9},{5,13},{9,1},{13,5},{2,10},{6,14},... | collective-permute-start | bytes 98312 | tf_op jit(solution)/shard_map/ppermute | solution.py:602
  19.1 0.0 copy-done.5
  19.1 2.1 %ready.1 = (bf16[2,2,256,256]{3,2,1,0:T(8,128)(2,1)S(1)}, f32[2,64,256]{2,1,0:T(8,128)S(1)}, f32[4,256,256]{2,1,0:T(8,128)S(1)}) custom-call(s32[2]{0:T(128)S(1)} %pad_add_fusion.bits, f32[64,256]{1,0:T(8,128)S(1)} %copy-done.5, f32[1024,256]{1,0:T(8,128)S(1)} %get-tuple-element.22.u, f32[256,256]{1,0:T(8,128)S(1)} %get-tuple-element.29.e_groups, ...), custom_call_target="tpu_custom_call" | custom-call | flops 3000000000 | tf_op jit(solution)/shard_map/ready/pallas_call | solution.py:486
  21.3 0.0 collective-permute-done.2.got
  21.3 4.7 %finish.1 = (f32[1024,256]{1,0:T(8,128)}, f32[1024,256]{1,0:T(8,128)}) custom-call(s32[2]{0:T(128)S(1)} %pad_add_fusion.bits, bf16[64,256]{1,0:T(8,128)(2,1)S(1)} %collective-permute-done.2.got, bf16[2,2,256,256]{3,2,1,0:T(8,128)(2,1)S(1)} %get-tuple-element.31.ready_ref, f32[2,64,256]{2,1,0:T(8,128)S(1)} %get-tuple-element.32.pre, ...), custom_call_target="tpu_custom_call" | custom-call | flops 3000000000 | tf_op jit(solution)/shard_map/finish/pallas_call | solution.py:565
Async XLA Ops:
  0.6 3.5 %copy-start.3 = (f32[256,256]{1,0:T(8,128)S(1)}, f32[256,256]{1,0:T(8,128)}, u32[]{:S(2)}) copy-start(f32[256,256]{1,0:T(8,128)} %ga.1) | copy-start | bytes 786436
  0.6 3.5 %copy-start.4 = (bf16[256,256]{1,0:T(8,128)(2,1)S(1)}, bf16[256,256]{1,0:T(8,128)(2,1)}, u32[]{:S(2)}) copy-start(bf16[256,256]{1,0:T(8,128)(2,1)} %tr.3) | copy-start | bytes 393220
  0.7 3.5 %copy-start.2 = (f32[256,256]{1,0:T(8,128)S(1)}, f32[256,256]{1,0:T(8,128)}, u32[]{:S(2)}) copy-start(f32[256,256]{1,0:T(8,128)} %loop.1) | copy-start | bytes 786436
  3.6 1.7 %copy-start = (bf16[128,16,512]{2,1,0:T(8,128)(2,1)S(1)}, bf16[128,16,512]{2,1,0:T(8,128)(2,1)}, u32[]{:S(2)}) copy-start(bf16[128,16,512]{2,1,0:T(8,128)(2,1)} %obs.3) | copy-start | bytes 6291460
  3.6 1.7 %copy-start.1 = (bf16[256,512]{1,0:T(8,128)(2,1)S(1)}, bf16[256,512]{1,0:T(8,128)(2,1)}, u32[]{:S(2)}) copy-start(bf16[256,512]{1,0:T(8,128)(2,1)} %gain.5) | copy-start | bytes 786436
  3.6 2.4 %collective-permute-start = (bf16[1024,256]{1,0:T(8,128)(2,1)}, bf16[1024,256]{1,0:T(8,128)(2,1)S(1)}, u32[]{:S(2)}, u32[]{:S(2)}) collective-permute-start(bf16[1024,256]{1,0:T(8,128)(2,1)} %other_inputs.1), channel_id=1, source_target_pairs={{0,1},{1,0},{2,3},{3,2},{4,5},{5,4},{6,7},{7,6},{8,9},{9,8},{10,11... | collective-permute-start | bytes 1572872 | tf_op jit(solution)/shard_map/ppermute | solution.py:593
  9.8 5.5 %collective-permute-start.1 = (bf16[64,512]{1,0:T(8,128)(2,1)S(1)}, bf16[64,512]{1,0:T(8,128)(2,1)S(1)}, u32[]{:S(2)}, u32[]{:S(2)}) collective-permute-start(bf16[64,512]{1,0:T(8,128)(2,1)S(1)} %get-tuple-element.25), channel_id=1, source_target_pairs={{0,4},{4,0},{8,12},{12,8},{1,5},{5,1},{9,13},{13,9},{2,6},{6,2},{1... | collective-permute-start | bytes 196616 | tf_op jit(solution)/shard_map/ppermute | solution.py:602
  15.3 3.8 %copy-start.5 = (f32[64,256]{1,0:T(8,128)S(1)}, f32[64,256]{1,0:T(8,128)}, u32[]{:S(2)}) copy-start(f32[64,256]{1,0:T(8,128)} %begin.1) | copy-start | bytes 196612
  16.2 5.0 %collective-permute-start.2 = (bf16[64,256]{1,0:T(8,128)(2,1)S(1)}, bf16[64,256]{1,0:T(8,128)(2,1)S(1)}, u32[]{:S(2)}, u32[]{:S(2)}) collective-permute-start(bf16[64,256]{1,0:T(8,128)(2,1)S(1)} %get-tuple-element.28), channel_id=1, source_target_pairs={{0,8},{4,12},{8,0},{12,4},{1,9},{5,13},{9,1},{13,5},{2,10},{6,14},... | collective-permute-start | bytes 98312 | tf_op jit(solution)/shard_map/ppermute | solution.py:602

commit v5 on v4

--- a/solution.py
+++ b/solution.py
@@ -8,6 +8,7 @@
 F32 = jnp.float32
 BF16 = jnp.bfloat16
 LANES = 128
+FEW = 64
 VMEM = pl.BlockSpec(memory_space=pltpu.VMEM)
 SMEM = pl.BlockSpec(memory_space=pltpu.SMEM)
 ANY = pl.BlockSpec(memory_space=pl.ANY)
@@ -33,6 +34,12 @@
 
 
 def muls(*terms):
+    rows = terms[0][0][0].shape[0]
+    if rows <= FEW:
+        both = jnp.concatenate([jnp.concatenate(x, 0) for x, _ in terms], 1)
+        high = jnp.concatenate([x[0] for x, _ in terms], 1)
+        result = dot(both, jnp.concatenate([y[0] for _, y in terms], 0))
+        return result[:rows] + result[rows:] + dot(high, jnp.concatenate([y[1] for _, y in terms], 0))
     left, right = [], []
     for x, y in terms:
         left += [x[0], x[1], x[0]]
@@ -358,11 +365,15 @@
     )(given, first)
 
 
-def sides(bit, mine, got):
+def bit(position, i):
+    return (position[0] >> i) & 1
+
+
+def sides(side, mine, got):
     states = mine.shape[2]
     got_e = got[:, pl.ds(0, states)].astype(F32)
     got_h = got[:, pl.ds(states, states)].astype(F32)
-    right = bit > 0
+    right = side > 0
     el, er = jnp.where(right, got_e, mine[0]), jnp.where(right, mine[0], got_e)
     hl, hr = jnp.where(right, got_h, mine[1]), jnp.where(right, mine[1], got_h)
     return el, er, hl, hr
@@ -371,7 +382,7 @@
 def join(level, names, bits, mine, got, mats):
     def kernel(bits, mine, got, mats_ref, ends, payload):
         m = Stack(names, mats_ref)
-        el, er, hl, hr = sides(bits[level], mine, got)
+        el, er, hl, hr = sides(bit(bits, level), mine, got)
         pair = halves(el)
         e = mul(pair, m["a"]) + er
         h = hl + muls((halves(hr), m["g"]), (pair, m["c"]))
@@ -395,12 +406,12 @@
 
     def kernel(bits, mine, got, mats_ref, top_ref, end, payload):
         m, t = Stack(names, mats_ref), Stack(TOP, top_ref)
-        el, er, hl, hr = sides(bits[level], mine, got)
+        el, er, hl, hr = sides(bit(bits, level), mine, got)
         pair = halves(el)
         e = er + mul(pair, m["a"])
         handed = hl + muls((halves(hr), m["g"]), (pair, t["c2"]), (halves(er), t["wg"]))
         end[0] = e
-        payload[...] = jnp.where(bits[level + 1] > 0, handed, e).astype(BF16)
+        payload[...] = jnp.where(bit(bits, level + 1) > 0, handed, e).astype(BF16)
 
     return pl.pallas_call(
         kernel,
@@ -439,8 +450,8 @@
         p, q, r, px, pd = unit, unit, none, zero, zero
         for i in range(top):
             m = level_maps[i]
-            right = bits[i] > 0
-            el, _, _, hr = sides(bits[i], mine[i], arrived[i])
+            right = bit(bits, i) > 0
+            el, _, _, hr = sides(bit(bits, i), mine[i], arrived[i])
             elp = halves(el)
             hand = mul(elp, m["k"]) + hr
             ak = halves(mul(m["a"], m["k"]))
@@ -459,7 +470,7 @@
                 )
                 p, q = either(right, halves(mul(m["a"], p)), p), either(right, q, halves(mul(m["g"], q)))
         m = level_maps[top]
-        right = bits[top] > 0
+        right = bit(bits, top) > 0
         w = f["w"]
         x0 = begin[...]
         own_e = mine[top][0]
@@ -498,11 +509,10 @@
     )(bits, begin, u, e_groups, mats_in, single, *maps, *ends, *got)
 
 
-def finish(bits, got, prepared, pre, local, x_groups, d_groups, mats, single, block, transition, gain):
+def finish(groups, bits, got, prepared, pre, local, x_groups, d_groups, mats, single, block, transition, gain):
     members, states = pre.shape[1:]
     quads = local.shape[1] // members
     steps = 4 * quads
-    groups = bits.shape[0]
 
     def kernel(bits, got, ready_ref, pre, local, xg, dg, mats_ref, single_ref, block_ref, tr, ga, *refs):
         filtered, smoothed, filtered_held, smoothed_held, sems = refs
@@ -523,9 +533,9 @@
         d = jnp.concatenate(ds + [d], 0)
         xp = halves(x)
         low = ga[...].astype(BF16)
-        final = bits[0] > 0
+        final = bit(bits, 0) > 0
         for i in range(1, groups):
-            final = jnp.logical_and(final, bits[i] > 0)
+            final = jnp.logical_and(final, bit(bits, i) > 0)
 
         def write(held, j, value):
             for q in range(quads):
@@ -586,8 +596,7 @@
     groups = blocks.bit_length() - 1
     assert blocks == 1 << groups and groups >= 2
     place = lax.axis_index("sens").astype(jnp.int32).reshape(1)
-    position = lax.axis_index("tm").astype(jnp.int32)
-    bits = jnp.stack([(position >> i) & 1 for i in range(groups)])
+    bits = lax.axis_index("tm").astype(jnp.int32).reshape(1)
 
     to_send = other_inputs(place, observations, obs_gain, members)
     other = lax.ppermute(to_send, "sens", [(0, 1), (1, 0)])
@@ -612,7 +621,7 @@
         bits, initial_mean, u, e_groups, mats, single, maps, mine, got[:-1]
     )
     filtered, smoothed = finish(
-        bits, got[-1], prepared, pre, local, x_groups, d_groups, mats, single, block, transition, smoother_gain
+        groups, bits, got[-1], prepared, pre, local, x_groups, d_groups, mats, single, block, transition, smoother_gain
     )
     shape = (members, steps, states)
     return filtered.reshape(shape), smoothed.reshape(shape)

time: 26.1 us -> 24.1 us (0.923)
  Pallas kernels: 18.6 us -> 16.6 us
    pallas_call x1, Pallas kernels: 4.66 us -> 3.86 us  [finish(): pl.pallas_call(kernel, out_shape=(jax.ShapeDtypeStruct((members * steps,...]
    pallas_call x1, Pallas kernels: 0.94 us -> 0.3 us  [last_join(): pl.pallas_call(kernel, out_shape=(jax.ShapeDtypeStruct((1, members, state...]
    pallas_call x1, Pallas kernels: 1.89 us -> 1.57 us  [up(): pl.pallas_call(kernel, out_shape=(jax.ShapeDtypeStruct((quads * members,...]
    pallas_call x1, Pallas kernels: 2.14 us -> 1.85 us  [ready(): pl.pallas_call(kernel, out_shape=(stack_shape(READY, states), jax.ShapeDt...]
  transfers between devices with their start and end apart: 3 -> 3, of which waited for: 0 -> 1; matrix products, arithmetic and copies ran while one was open for 0% -> 0% of each run, Pallas kernels for 25% -> 25%
where the time goes in v5:
time: 24.1 us; the launch traced here: 23.9 us
  Pallas kernels  16.6 us (69%)
  starting transfers between devices  6.38 us (26%)
  between operations  0.77 us (3%)
    ppermute x2, starting transfers between devices, body(): lax.ppermute(payload, 'tm', [(j, j ^ 1 << i) for j in range(blocks)])  5.86 us
    pallas_call x1, Pallas kernels, finish(): pl.pallas_call(kernel, out_shape=(jax.ShapeDtypeStruct((members * steps,...  3.86 us
    pallas_call x1, Pallas kernels, other_inputs(): pl.pallas_call(kernel, out_shape=jax.ShapeDtypeStruct((rows, states), BF1...  2.92 us
    pallas_call x1, Pallas kernels, all_maps(): pl.pallas_call(both_kernel if joined else kernel, out_shape=shapes, in_sp...  2.44 us
    pallas_call x1, Pallas kernels, second_powers(): pl.pallas_call(kernel, out_shape=(stack_shape(SECOND, n), jax.ShapeDtypeS...  1.85 us
    pallas_call x1, Pallas kernels, ready(): pl.pallas_call(kernel, out_shape=(stack_shape(READY, states), jax.ShapeDt...  1.85 us
    pallas_call x1, Pallas kernels, up(): pl.pallas_call(kernel, out_shape=(jax.ShapeDtypeStruct((quads * members,...  1.57 us
    pallas_call x1, Pallas kernels, first_powers(): pl.pallas_call(kernel, out_shape=(stack_shape(FIRST, n), jax.ShapeDtypeSt...  1.1 us
  transfers between devices with their start and end apart: 3, of which 1 were waited for; matrix products, arithmetic and copies ran while one was open for 0% of the time, Pallas kernels for 25%

profile of v5, /device:TPU:0, one launch (start us, length us, event | category | flops | bytes accessed | tf_op | source)
XLA Modules:
  0.0 23.9 jit_solution(17559868206744034502)
XLA Ops:
  0.6 0.0 copy-start.3
  0.6 0.0 copy-start.4
  0.7 0.0 copy-start.2
  0.7 2.9 %other_inputs.1 = bf16[1024,256]{1,0:T(8,128)(2,1)} custom-call(s32[1]{0:T(128)} %bitcast.1.place, bf16[128,16,512]{2,1,0:T(8,128)(2,1)} %obs.3, bf16[256,512]{1,0:T(8,128)(2,1)} %gain.5), custom_call_target="tpu_custom_call" | custom-call | flops 500000000 | tf_op jit(solution)/shard_map/other_inputs/pallas_call | solution.py:196
  3.6 0.0 copy-start
  3.6 0.0 copy-start.1
  3.6 0.5 %collective-permute-start = (bf16[1024,256]{1,0:T(8,128)(2,1)}, bf16[1024,256]{1,0:T(8,128)(2,1)S(1)}, u32[]{:S(2)}, u32[]{:S(2)}) collective-permute-start(bf16[1024,256]{1,0:T(8,128)(2,1)} %other_inputs.1), channel_id=1, source_target_pairs={{0,1},{1,0},{2,3},{3,2},{4,5},{5,4},{6,7},{7,6},{8,9},{9,8},{10,11... | collective-permute-start | bytes 1572872 | tf_op jit(solution)/shard_map/ppermute | solution.py:602
  4.1 0.0 copy-done.3
  4.1 0.0 copy-done.4
  4.1 0.0 copy-done.2
  4.1 1.1 %first_powers.1 = (bf16[10,2,256,256]{3,2,1,0:T(8,128)(2,1)S(1)}, f32[8,128]{1,0:T(8,128)S(1)}) custom-call(f32[256,256]{1,0:T(8,128)S(1)} %copy-done.2, f32[256,256]{1,0:T(8,128)S(1)} %copy-done.3, bf16[256,256]{1,0:T(8,128)(2,1)S(1)} %copy-done.4), custom_call_target="tpu_custom_call" | custom-call | flops 1000000000 | tf_op jit(solution)/shard_map/first_powers/pallas_call | solution.py:128
  5.2 0.0 copy-done
  5.3 0.0 copy-done.1
  5.3 0.7 %own_inputs.1.own = f32[1024,256]{1,0:T(8,128)S(1)} custom-call(s32[1]{0:T(128)} %bitcast.1.place, bf16[128,16,512]{2,1,0:T(8,128)(2,1)S(1)} %copy-done, bf16[256,512]{1,0:T(8,128)(2,1)S(1)} %copy-done.1, f32[8,128]{1,0:T(8,128)S(1)} %get-tuple-element.21._), custom_call_target="tpu_custom_call" | custom-call | flops 500000000 | tf_op jit(solution)/shard_map/own_inputs/pallas_call | solution.py:225
  6.0 0.0 collective-permute-done.other
  6.0 1.9 %second_powers.1 = (bf16[9,2,256,256]{3,2,1,0:T(8,128)(2,1)S(1)}, f32[1024,256]{1,0:T(8,128)S(1)}) custom-call(bf16[10,2,256,256]{3,2,1,0:T(8,128)(2,1)S(1)} %get-tuple-element.20.first_ref.mats_ref, f32[1024,256]{1,0:T(8,128)S(1)} %own_inputs.1.own, bf16[1024,256]{1,0:T(8,128)(2,1)S(1)} %collective-permute-done.other), custom_call_target="tpu_custom_call" | custom-call | flops 1500000000 | tf_op jit(solution)/shard_map/second_powers/pallas_call | solution.py:161
  7.9 1.6 %up.1 = (f32[256,256]{1,0:T(8,128)S(1)}, f32[192,256]{1,0:T(8,128)S(1)}, f32[192,256]{1,0:T(8,128)S(1)}, f32[2,64,256]{2,1,0:T(8,128)S(1)}, bf16[64,512]{1,0:T(8,128)(2,1)S(1)}) custom-call(f32[1024,256]{1,0:T(8,128)S(1)} %get-tuple-element.22.u, bf16[10,2,256,256]{3,2,1,0:T(8,128)(2,1)S(1)} %get-tuple-element.20.first_ref.mats_ref, ...), custom_call_target="tpu_custom_call" | custom-call | flops 2000000000 | tf_op jit(solution)/shard_map/up/pallas_call | solution.py:275
  9.4 3.0 %collective-permute-start.1 = (bf16[64,512]{1,0:T(8,128)(2,1)S(1)}, bf16[64,512]{1,0:T(8,128)(2,1)S(1)}, u32[]{:S(2)}, u32[]{:S(2)}) collective-permute-start(bf16[64,512]{1,0:T(8,128)(2,1)S(1)} %get-tuple-element.25), channel_id=1, source_target_pairs={{0,4},{4,0},{8,12},{12,8},{1,5},{5,1},{9,13},{13,9},{2,6},{6,2},{1... | collective-permute-start | bytes 196616 | tf_op jit(solution)/shard_map/ppermute | solution.py:611
  12.4 2.4 %block_maps.1 = (bf16[7,2,256,256]{3,2,1,0:T(8,128)(2,1)S(1)}, bf16[5,2,256,256]{3,2,1,0:T(8,128)(2,1)S(1)}) custom-call(bf16[10,2,256,256]{3,2,1,0:T(8,128)(2,1)S(1)} %get-tuple-element.20.first_ref.mats_ref, bf16[9,2,256,256]{3,2,1,0:T(8,128)(2,1)S(1)} %get-tuple-element.23.second_ref.single_ref, f32[2,64,256]{2,1,0:T(8,128)S(1)} %get-tuple-element.24._.mine.refs_2_), custom_call_target="tpu_custom_call" | custom-call | flops 1200000000 | tf_op jit(solution)/shard_map/block_maps/pallas_call | solution.py:335
  14.9 0.0 copy-start.5
  14.9 0.0 collective-permute-done.1.got.refs_4_
  14.9 0.3 %last_join.1 = (f32[1,64,256]{2,1,0:T(8,128)S(1)}, bf16[64,256]{1,0:T(8,128)(2,1)S(1)}) custom-call(s32[1]{0:T(128)} %bitcast.bits, f32[2,64,256]{2,1,0:T(8,128)S(1)} %get-tuple-element.24._.mine.refs_2_, bf16[64,512]{1,0:T(8,128)(2,1)S(1)} %collective-permute-done.1.got.refs_4_, bf16[7,2,256,256]{3,2,1,0:T(8,128)(2,1)S(1)} %get-tuple-element.26.mats_ref.refs_0_.block_ref, ...), custom_call_target="tpu_custom_call" | custom-call | flops 100000000 | tf_op jit(solution)/shard_map/last_join/pallas_call | solution.py:416
  15.2 2.9 %collective-permute-start.2 = (bf16[64,256]{1,0:T(8,128)(2,1)S(1)}, bf16[64,256]{1,0:T(8,128)(2,1)S(1)}, u32[]{:S(2)}, u32[]{:S(2)}) collective-permute-start(bf16[64,256]{1,0:T(8,128)(2,1)S(1)} %get-tuple-element.28), channel_id=1, source_target_pairs={{0,8},{4,12},{8,0},{12,4},{1,9},{5,13},{9,1},{13,5},{2,10},{6,14},... | collective-permute-start | bytes 98312 | tf_op jit(solution)/shard_map/ppermute | solution.py:611
  18.1 0.0 copy-done.5
  18.1 1.8 %ready.1 = (bf16[2,2,256,256]{3,2,1,0:T(8,128)(2,1)S(1)}, f32[2,64,256]{2,1,0:T(8,128)S(1)}, f32[4,256,256]{2,1,0:T(8,128)S(1)}) custom-call(s32[1]{0:T(128)} %bitcast.bits, f32[64,256]{1,0:T(8,128)S(1)} %copy-done.5, f32[1024,256]{1,0:T(8,128)S(1)} %get-tuple-element.22.u, f32[256,256]{1,0:T(8,128)S(1)} %get-tuple-element.29.e_groups, ...), custom_call_target="tpu_custom_call" | custom-call | flops 3000000000 | tf_op jit(solution)/shard_map/ready/pallas_call | solution.py:497
  19.9 0.2 collective-permute-done.2.got
  20.1 3.9 %finish.1 = (f32[1024,256]{1,0:T(8,128)}, f32[1024,256]{1,0:T(8,128)}) custom-call(s32[1]{0:T(128)} %bitcast.bits, bf16[64,256]{1,0:T(8,128)(2,1)S(1)} %collective-permute-done.2.got, bf16[2,2,256,256]{3,2,1,0:T(8,128)(2,1)S(1)} %get-tuple-element.31.ready_ref, f32[2,64,256]{2,1,0:T(8,128)S(1)} %get-tuple-element.32.pre, ...), custom_call_target="tpu_custom_call" | custom-call | flops 3000000000 | tf_op jit(solution)/shard_map/finish/pallas_call | solution.py:575
Async XLA Ops:
  0.6 3.5 %copy-start.3 = (f32[256,256]{1,0:T(8,128)S(1)}, f32[256,256]{1,0:T(8,128)}, u32[]{:S(2)}) copy-start(f32[256,256]{1,0:T(8,128)} %ga.1) | copy-start | bytes 786436
  0.6 3.5 %copy-start.4 = (bf16[256,256]{1,0:T(8,128)(2,1)S(1)}, bf16[256,256]{1,0:T(8,128)(2,1)}, u32[]{:S(2)}) copy-start(bf16[256,256]{1,0:T(8,128)(2,1)} %tr.3) | copy-start | bytes 393220
  0.7 3.5 %copy-start.2 = (f32[256,256]{1,0:T(8,128)S(1)}, f32[256,256]{1,0:T(8,128)}, u32[]{:S(2)}) copy-start(f32[256,256]{1,0:T(8,128)} %loop.1) | copy-start | bytes 786436
  3.6 1.7 %copy-start = (bf16[128,16,512]{2,1,0:T(8,128)(2,1)S(1)}, bf16[128,16,512]{2,1,0:T(8,128)(2,1)}, u32[]{:S(2)}) copy-start(bf16[128,16,512]{2,1,0:T(8,128)(2,1)} %obs.3) | copy-start | bytes 6291460
  3.6 1.7 %copy-start.1 = (bf16[256,512]{1,0:T(8,128)(2,1)S(1)}, bf16[256,512]{1,0:T(8,128)(2,1)}, u32[]{:S(2)}) copy-start(bf16[256,512]{1,0:T(8,128)(2,1)} %gain.5) | copy-start | bytes 786436
  3.6 2.4 %collective-permute-start = (bf16[1024,256]{1,0:T(8,128)(2,1)}, bf16[1024,256]{1,0:T(8,128)(2,1)S(1)}, u32[]{:S(2)}, u32[]{:S(2)}) collective-permute-start(bf16[1024,256]{1,0:T(8,128)(2,1)} %other_inputs.1), channel_id=1, source_target_pairs={{0,1},{1,0},{2,3},{3,2},{4,5},{5,4},{6,7},{7,6},{8,9},{9,8},{10,11... | collective-permute-start | bytes 1572872 | tf_op jit(solution)/shard_map/ppermute | solution.py:602
  9.4 5.5 %collective-permute-start.1 = (bf16[64,512]{1,0:T(8,128)(2,1)S(1)}, bf16[64,512]{1,0:T(8,128)(2,1)S(1)}, u32[]{:S(2)}, u32[]{:S(2)}) collective-permute-start(bf16[64,512]{1,0:T(8,128)(2,1)S(1)} %get-tuple-element.25), channel_id=1, source_target_pairs={{0,4},{4,0},{8,12},{12,8},{1,5},{5,1},{9,13},{13,9},{2,6},{6,2},{1... | collective-permute-start | bytes 196616 | tf_op jit(solution)/shard_map/ppermute | solution.py:611
  14.9 3.2 %copy-start.5 = (f32[64,256]{1,0:T(8,128)S(1)}, f32[64,256]{1,0:T(8,128)}, u32[]{:S(2)}) copy-start(f32[64,256]{1,0:T(8,128)} %begin.1) | copy-start | bytes 196612
  15.2 4.9 %collective-permute-start.2 = (bf16[64,256]{1,0:T(8,128)(2,1)S(1)}, bf16[64,256]{1,0:T(8,128)(2,1)S(1)}, u32[]{:S(2)}, u32[]{:S(2)}) collective-permute-start(bf16[64,256]{1,0:T(8,128)(2,1)S(1)} %get-tuple-element.28), channel_id=1, source_target_pairs={{0,8},{4,12},{8,0},{12,4},{1,9},{5,13},{9,1},{13,5},{2,10},{6,14},... | collective-permute-start | bytes 98312 | tf_op jit(solution)/shard_map/ppermute | solution.py:611

commit v6 on v5

--- a/solution.py
+++ b/solution.py
@@ -8,7 +8,7 @@
 F32 = jnp.float32
 BF16 = jnp.bfloat16
 LANES = 128
-FEW = 64
+FEW = 256
 VMEM = pl.BlockSpec(memory_space=pltpu.VMEM)
 SMEM = pl.BlockSpec(memory_space=pltpu.SMEM)
 ANY = pl.BlockSpec(memory_space=pl.ANY)

time: 24.1 us -> 24 us (level)
  no operation moved by 1% of the time
where the time goes in v6:
time: 24 us; the launch traced here: 23.9 us
  Pallas kernels  16.5 us (69%)
  starting transfers between devices  6.42 us (27%)
  between operations  0.78 us (3%)
    ppermute x2, starting transfers between devices, body(): lax.ppermute(payload, 'tm', [(j, j ^ 1 << i) for j in range(blocks)])  5.9 us
    pallas_call x1, Pallas kernels, finish(): pl.pallas_call(kernel, out_shape=(jax.ShapeDtypeStruct((members * steps,...  3.85 us
    pallas_call x1, Pallas kernels, other_inputs(): pl.pallas_call(kernel, out_shape=jax.ShapeDtypeStruct((rows, states), BF1...  2.92 us
    pallas_call x1, Pallas kernels, all_maps(): pl.pallas_call(both_kernel if joined else kernel, out_shape=shapes, in_sp...  2.43 us
    pallas_call x1, Pallas kernels, ready(): pl.pallas_call(kernel, out_shape=(stack_shape(READY, states), jax.ShapeDt...  1.83 us
    pallas_call x1, Pallas kernels, second_powers(): pl.pallas_call(kernel, out_shape=(stack_shape(SECOND, n), jax.ShapeDtypeS...  1.81 us
    pallas_call x1, Pallas kernels, up(): pl.pallas_call(kernel, out_shape=(jax.ShapeDtypeStruct((quads * members,...  1.55 us
    pallas_call x1, Pallas kernels, first_powers(): pl.pallas_call(kernel, out_shape=(stack_shape(FIRST, n), jax.ShapeDtypeSt...  1.09 us
  transfers between devices with their start and end apart: 3, of which 1 were waited for; matrix products, arithmetic and copies ran while one was open for 0% of the time, Pallas kernels for 25%

profile of v6, /device:TPU:0, one launch (start us, length us, event | category | flops | bytes accessed | tf_op | source)
XLA Modules:
  0.0 23.9 jit_solution(4562794410927713008)
XLA Ops:
  0.6 0.0 copy-start.3
  0.6 0.0 copy-start.4
  0.7 0.0 copy-start.2
  0.7 2.9 %other_inputs.1 = bf16[1024,256]{1,0:T(8,128)(2,1)} custom-call(s32[1]{0:T(128)} %bitcast.1.place, bf16[128,16,512]{2,1,0:T(8,128)(2,1)} %obs.3, bf16[256,512]{1,0:T(8,128)(2,1)} %gain.5), custom_call_target="tpu_custom_call" | custom-call | flops 500000000 | tf_op jit(solution)/shard_map/other_inputs/pallas_call | solution.py:196
  3.6 0.0 copy-start
  3.6 0.0 copy-start.1
  3.6 0.5 %collective-permute-start = (bf16[1024,256]{1,0:T(8,128)(2,1)}, bf16[1024,256]{1,0:T(8,128)(2,1)S(1)}, u32[]{:S(2)}, u32[]{:S(2)}) collective-permute-start(bf16[1024,256]{1,0:T(8,128)(2,1)} %other_inputs.1), channel_id=1, source_target_pairs={{0,1},{1,0},{2,3},{3,2},{4,5},{5,4},{6,7},{7,6},{8,9},{9,8},{10,11... | collective-permute-start | bytes 1572872 | tf_op jit(solution)/shard_map/ppermute | solution.py:602
  4.1 0.0 copy-done.3
  4.1 0.0 copy-done.4
  4.1 0.0 copy-done.2
  4.1 1.1 %first_powers.1 = (bf16[10,2,256,256]{3,2,1,0:T(8,128)(2,1)S(1)}, f32[8,128]{1,0:T(8,128)S(1)}) custom-call(f32[256,256]{1,0:T(8,128)S(1)} %copy-done.2, f32[256,256]{1,0:T(8,128)S(1)} %copy-done.3, bf16[256,256]{1,0:T(8,128)(2,1)S(1)} %copy-done.4), custom_call_target="tpu_custom_call" | custom-call | flops 1000000000 | tf_op jit(solution)/shard_map/first_powers/pallas_call | solution.py:128
  5.2 0.0 copy-done
  5.3 0.0 copy-done.1
  5.3 0.7 %own_inputs.1.own = f32[1024,256]{1,0:T(8,128)S(1)} custom-call(s32[1]{0:T(128)} %bitcast.1.place, bf16[128,16,512]{2,1,0:T(8,128)(2,1)S(1)} %copy-done, bf16[256,512]{1,0:T(8,128)(2,1)S(1)} %copy-done.1, f32[8,128]{1,0:T(8,128)S(1)} %get-tuple-element.21._), custom_call_target="tpu_custom_call" | custom-call | flops 500000000 | tf_op jit(solution)/shard_map/own_inputs/pallas_call | solution.py:225
  6.0 0.0 collective-permute-done.other
  6.0 1.8 %second_powers.1 = (bf16[9,2,256,256]{3,2,1,0:T(8,128)(2,1)S(1)}, f32[1024,256]{1,0:T(8,128)S(1)}) custom-call(bf16[10,2,256,256]{3,2,1,0:T(8,128)(2,1)S(1)} %get-tuple-element.20.first_ref.mats_ref, f32[1024,256]{1,0:T(8,128)S(1)} %own_inputs.1.own, bf16[1024,256]{1,0:T(8,128)(2,1)S(1)} %collective-permute-done.other), custom_call_target="tpu_custom_call" | custom-call | flops 1500000000 | tf_op jit(solution)/shard_map/second_powers/pallas_call | solution.py:161
  7.8 1.5 %up.1 = (f32[256,256]{1,0:T(8,128)S(1)}, f32[192,256]{1,0:T(8,128)S(1)}, f32[192,256]{1,0:T(8,128)S(1)}, f32[2,64,256]{2,1,0:T(8,128)S(1)}, bf16[64,512]{1,0:T(8,128)(2,1)S(1)}) custom-call(f32[1024,256]{1,0:T(8,128)S(1)} %get-tuple-element.22.u, bf16[10,2,256,256]{3,2,1,0:T(8,128)(2,1)S(1)} %get-tuple-element.20.first_ref.mats_ref, ...), custom_call_target="tpu_custom_call" | custom-call | flops 2000000000 | tf_op jit(solution)/shard_map/up/pallas_call | solution.py:275
  9.4 3.0 %collective-permute-start.1 = (bf16[64,512]{1,0:T(8,128)(2,1)S(1)}, bf16[64,512]{1,0:T(8,128)(2,1)S(1)}, u32[]{:S(2)}, u32[]{:S(2)}) collective-permute-start(bf16[64,512]{1,0:T(8,128)(2,1)S(1)} %get-tuple-element.25), channel_id=1, source_target_pairs={{0,4},{4,0},{8,12},{12,8},{1,5},{5,1},{9,13},{13,9},{2,6},{6,2},{1... | collective-permute-start | bytes 196616 | tf_op jit(solution)/shard_map/ppermute | solution.py:611
  12.4 2.4 %block_maps.1 = (bf16[7,2,256,256]{3,2,1,0:T(8,128)(2,1)S(1)}, bf16[5,2,256,256]{3,2,1,0:T(8,128)(2,1)S(1)}) custom-call(bf16[10,2,256,256]{3,2,1,0:T(8,128)(2,1)S(1)} %get-tuple-element.20.first_ref.mats_ref, bf16[9,2,256,256]{3,2,1,0:T(8,128)(2,1)S(1)} %get-tuple-element.23.second_ref.single_ref, f32[2,64,256]{2,1,0:T(8,128)S(1)} %get-tuple-element.24._.mine.refs_2_), custom_call_target="tpu_custom_call" | custom-call | flops 1200000000 | tf_op jit(solution)/shard_map/block_maps/pallas_call | solution.py:335
  14.8 0.0 copy-start.5
  14.8 0.0 collective-permute-done.1.got.refs_4_
  14.8 0.3 %last_join.1 = (f32[1,64,256]{2,1,0:T(8,128)S(1)}, bf16[64,256]{1,0:T(8,128)(2,1)S(1)}) custom-call(s32[1]{0:T(128)} %bitcast.bits, f32[2,64,256]{2,1,0:T(8,128)S(1)} %get-tuple-element.24._.mine.refs_2_, bf16[64,512]{1,0:T(8,128)(2,1)S(1)} %collective-permute-done.1.got.refs_4_, bf16[7,2,256,256]{3,2,1,0:T(8,128)(2,1)S(1)} %get-tuple-element.26.mats_ref.refs_0_.block_ref, ...), custom_call_target="tpu_custom_call" | custom-call | flops 100000000 | tf_op jit(solution)/shard_map/last_join/pallas_call | solution.py:416
  15.1 2.9 %collective-permute-start.2 = (bf16[64,256]{1,0:T(8,128)(2,1)S(1)}, bf16[64,256]{1,0:T(8,128)(2,1)S(1)}, u32[]{:S(2)}, u32[]{:S(2)}) collective-permute-start(bf16[64,256]{1,0:T(8,128)(2,1)S(1)} %get-tuple-element.28), channel_id=1, source_target_pairs={{0,8},{4,12},{8,0},{12,4},{1,9},{5,13},{9,1},{13,5},{2,10},{6,14},... | collective-permute-start | bytes 98312 | tf_op jit(solution)/shard_map/ppermute | solution.py:611
  18.0 0.0 copy-done.5
  18.0 1.8 %ready.1 = (bf16[2,2,256,256]{3,2,1,0:T(8,128)(2,1)S(1)}, f32[2,64,256]{2,1,0:T(8,128)S(1)}, f32[4,256,256]{2,1,0:T(8,128)S(1)}) custom-call(s32[1]{0:T(128)} %bitcast.bits, f32[64,256]{1,0:T(8,128)S(1)} %copy-done.5, f32[1024,256]{1,0:T(8,128)S(1)} %get-tuple-element.22.u, f32[256,256]{1,0:T(8,128)S(1)} %get-tuple-element.29.e_groups, ...), custom_call_target="tpu_custom_call" | custom-call | flops 3000000000 | tf_op jit(solution)/shard_map/ready/pallas_call | solution.py:497
  19.9 0.2 collective-permute-done.2.got
  20.0 3.9 %finish.1 = (f32[1024,256]{1,0:T(8,128)}, f32[1024,256]{1,0:T(8,128)}) custom-call(s32[1]{0:T(128)} %bitcast.bits, bf16[64,256]{1,0:T(8,128)(2,1)S(1)} %collective-permute-done.2.got, bf16[2,2,256,256]{3,2,1,0:T(8,128)(2,1)S(1)} %get-tuple-element.31.ready_ref, f32[2,64,256]{2,1,0:T(8,128)S(1)} %get-tuple-element.32.pre, ...), custom_call_target="tpu_custom_call" | custom-call | flops 3000000000 | tf_op jit(solution)/shard_map/finish/pallas_call | solution.py:575
Async XLA Ops:
  0.6 3.5 %copy-start.3 = (f32[256,256]{1,0:T(8,128)S(1)}, f32[256,256]{1,0:T(8,128)}, u32[]{:S(2)}) copy-start(f32[256,256]{1,0:T(8,128)} %ga.1) | copy-start | bytes 786436
  0.6 3.5 %copy-start.4 = (bf16[256,256]{1,0:T(8,128)(2,1)S(1)}, bf16[256,256]{1,0:T(8,128)(2,1)}, u32[]{:S(2)}) copy-start(bf16[256,256]{1,0:T(8,128)(2,1)} %tr.3) | copy-start | bytes 393220
  0.7 3.5 %copy-start.2 = (f32[256,256]{1,0:T(8,128)S(1)}, f32[256,256]{1,0:T(8,128)}, u32[]{:S(2)}) copy-start(f32[256,256]{1,0:T(8,128)} %loop.1) | copy-start | bytes 786436
  3.6 1.7 %copy-start = (bf16[128,16,512]{2,1,0:T(8,128)(2,1)S(1)}, bf16[128,16,512]{2,1,0:T(8,128)(2,1)}, u32[]{:S(2)}) copy-start(bf16[128,16,512]{2,1,0:T(8,128)(2,1)} %obs.3) | copy-start | bytes 6291460
  3.6 1.7 %copy-start.1 = (bf16[256,512]{1,0:T(8,128)(2,1)S(1)}, bf16[256,512]{1,0:T(8,128)(2,1)}, u32[]{:S(2)}) copy-start(bf16[256,512]{1,0:T(8,128)(2,1)} %gain.5) | copy-start | bytes 786436
  3.6 2.4 %collective-permute-start = (bf16[1024,256]{1,0:T(8,128)(2,1)}, bf16[1024,256]{1,0:T(8,128)(2,1)S(1)}, u32[]{:S(2)}, u32[]{:S(2)}) collective-permute-start(bf16[1024,256]{1,0:T(8,128)(2,1)} %other_inputs.1), channel_id=1, source_target_pairs={{0,1},{1,0},{2,3},{3,2},{4,5},{5,4},{6,7},{7,6},{8,9},{9,8},{10,11... | collective-permute-start | bytes 1572872 | tf_op jit(solution)/shard_map/ppermute | solution.py:602
  9.4 5.5 %collective-permute-start.1 = (bf16[64,512]{1,0:T(8,128)(2,1)S(1)}, bf16[64,512]{1,0:T(8,128)(2,1)S(1)}, u32[]{:S(2)}, u32[]{:S(2)}) collective-permute-start(bf16[64,512]{1,0:T(8,128)(2,1)S(1)} %get-tuple-element.25), channel_id=1, source_target_pairs={{0,4},{4,0},{8,12},{12,8},{1,5},{5,1},{9,13},{13,9},{2,6},{6,2},{1... | collective-permute-start | bytes 196616 | tf_op jit(solution)/shard_map/ppermute | solution.py:611
  14.8 3.2 %copy-start.5 = (f32[64,256]{1,0:T(8,128)S(1)}, f32[64,256]{1,0:T(8,128)}, u32[]{:S(2)}) copy-start(f32[64,256]{1,0:T(8,128)} %begin.1) | copy-start | bytes 196612
  15.1 4.9 %collective-permute-start.2 = (bf16[64,256]{1,0:T(8,128)(2,1)S(1)}, bf16[64,256]{1,0:T(8,128)(2,1)S(1)}, u32[]{:S(2)}, u32[]{:S(2)}) collective-permute-start(bf16[64,256]{1,0:T(8,128)(2,1)S(1)} %get-tuple-element.28), channel_id=1, source_target_pairs={{0,8},{4,12},{8,0},{12,4},{1,9},{5,13},{9,1},{13,5},{2,10},{6,14},... | collective-permute-start | bytes 98312 | tf_op jit(solution)/shard_map/ppermute | solution.py:611
